TPU v7x, 512 devices: a whole 4x8x8 slice. The times are simulated.
512 devices in a mesh: dp: 128 (over y_lo, z, x, core), tensor: 4 (over y_hi).
Axes of the slice: x: 4, y: 8 (y_hi: 4, y_lo: 2; y = y_hi * 2 + y_lo), z: 8, core: 2. Of those that a mesh axis runs over, the one named last changes fastest.
Arguments:
- pooled_caption_states: bfloat16 [8192, 1152], P('dp', 'tensor'), may hold values from -6 to 6
- first_dense_matrix: bfloat16 [1152, 3072], P(None, 'tensor'), may hold values from -0.1875 to 0.1875
- first_dense_offset: float32 [3072], P('tensor'), may hold values from -4 to 4
- second_dense_matrix: bfloat16 [3072, 1152], P('tensor'), may hold values from -0.109375 to 0.109375
- second_dense_offset: float32 [1152], replicated, may hold values from -4 to 4
- picture_vectors_unnormed: bfloat16 [8192, 1152], P('dp'), may hold values from -6 to 6
- matching_caption_position: int32 [8192], P('dp'), may hold values from 0 to 8191, each once
- learned_sharpness: float32 [1], replicated, may hold values from 5 to 20
- learned_score_offset: float32 [1], replicated, may hold values from -5 to -2
Outputs:
- text_grad: float32 [8192, 1152], P(('dp', 'tensor'))
- image_grad: float32 [8192, 1152], P(('dp', 'tensor'))
Inputs may be any that keep to these rules, and one draw needn't show every extreme that they name: matching_caption_position is a permutation: every text row is the positive of exactly one image.
All inputs are finite; a program needn't handle non-finite values.
Results may differ from a plain program's by a relative error of at most 0.004.
Values may be sent and summed in bfloat16 or wider, within the bound.
No kernel may reach another device: no remote copies, remote signals or barrier semaphores. Data moves between devices by JAX's collectives and lax.ppermute only.
A program may use at most 64 MiB of HBM per device.

v0:
```python
import jax
import jax.numpy as jnp
from jax import lax
from jax.sharding import PartitionSpec as P

EPSILON = 1e-06


def from_behind(shard, axis, by):
    length = lax.axis_size(axis)
    return lax.ppermute(shard, axis, [(i, (i + by) % length) for i in range(length)])


def layer_norm(values):
    widened = values.astype(jnp.float32)
    centred = widened - jnp.mean(widened, axis=-1, keepdims=True)
    variance = jnp.mean(centred * centred, axis=-1, keepdims=True)
    return (centred * lax.rsqrt(variance + EPSILON)).astype(jnp.bfloat16)


def unit_rows(values):
    squared = jnp.sum(values * values, axis=-1, keepdims=True)
    return (values * lax.rsqrt(squared + EPSILON)).astype(jnp.bfloat16)


def couple_losses(
    layer_group,
    group_numbers,
    picture_direction,
    matching_caption_position,
    sharpness_factor,
    additive_constant,
):
    similarity_matrix = (
        sharpness_factor
        * lax.dot_general(
            layer_group,
            picture_direction,
            (((1,), (1,)), ((), ())),
            preferred_element_type=jnp.float32,
        )
        + additive_constant
    )
    matched = matching_caption_position[None, :] == group_numbers[:, None]
    label_sign_matrix = jnp.where(matched, 1.0, -1.0).astype(jnp.float32)
    sigmoid_coefficients = (
        -sharpness_factor
        * label_sign_matrix
        * jax.nn.sigmoid(-label_sign_matrix * similarity_matrix)
    ).astype(jnp.bfloat16)
    caption_share = jnp.dot(
        sigmoid_coefficients, picture_direction, preferred_element_type=jnp.float32
    )
    picture_share = lax.dot_general(
        sigmoid_coefficients,
        layer_group,
        (((0,), (0,)), ((), ())),
        preferred_element_type=jnp.float32,
    )
    return (caption_share, picture_share)


def advance_text(layer_group):
    return from_behind(layer_group, "dp", 1)


def advance_grad(grads):
    return from_behind(grads, "dp", 1)


def shards(
    pooled_caption_states,
    first_dense_matrix,
    first_dense_offset,
    second_dense_matrix,
    second_dense_offset,
    picture_vectors_unnormed,
    matching_caption_position,
    learned_sharpness,
    learned_score_offset,
):
    gathered = lax.all_gather(pooled_caption_states, "tensor", axis=1, tiled=True)
    normed = layer_norm(gathered)
    hidden = jax.nn.gelu(
        jnp.dot(normed, first_dense_matrix, preferred_element_type=jnp.float32)
        + first_dense_offset,
        approximate=True,
    ).astype(jnp.bfloat16)
    group_rows = gathered.shape[0]
    width = gathered.shape[1]
    tensor_count = lax.axis_size("tensor")
    own_rows = group_rows // tensor_count
    tensor_pos = lax.axis_index("tensor")
    summed = lax.psum(
        jnp.dot(hidden, second_dense_matrix, preferred_element_type=jnp.float32), "tensor"
    )
    branch = lax.dynamic_slice_in_dim(summed, tensor_pos * own_rows, own_rows, 0)
    residual_rows = lax.dynamic_slice_in_dim(gathered, tensor_pos * own_rows, own_rows, 0).astype(
        jnp.float32
    )
    text_unit = unit_rows(residual_rows + branch + second_dense_offset)
    picture_direction = unit_rows(picture_vectors_unnormed.astype(jnp.float32))
    sharpness_factor = learned_sharpness[0]
    additive_constant = learned_score_offset[0]
    cycle_size = lax.axis_size("dp")
    cycle_pos = lax.axis_index("dp")
    image_start = jnp.zeros((group_rows, width), jnp.float32)

    def text_ids(anchor, count_rows):
        return (anchor * tensor_count + tensor_pos) * own_rows + jnp.arange(
            count_rows, dtype=jnp.int32
        )

    def one_step(step, carry):
        layer_group, grads, image_total = carry
        anchor = (cycle_pos - step) % cycle_size
        caption_share, picture_share = couple_losses(
            layer_group,
            text_ids(anchor, own_rows),
            picture_direction,
            matching_caption_position,
            sharpness_factor,
            additive_constant,
        )
        return (
            advance_text(layer_group),
            advance_grad(grads + caption_share),
            image_total + picture_share,
        )

    start_grads = jnp.zeros((own_rows, width), jnp.float32)
    layer_group, grads, image_total = lax.fori_loop(
        0, cycle_size - 1, one_step, (text_unit, start_grads, image_start)
    )
    last_anchor = (cycle_pos + 1) % cycle_size
    caption_share, picture_share = couple_losses(
        layer_group,
        text_ids(last_anchor, own_rows),
        picture_direction,
        matching_caption_position,
        sharpness_factor,
        additive_constant,
    )
    text_grad = advance_grad(grads + caption_share)
    image_total = image_total + picture_share
    image_grad = lax.psum_scatter(image_total, "tensor", scatter_dimension=0, tiled=True)
    return (text_grad, image_grad)


def solution(mesh):
    return jax.shard_map(
        shards,
        mesh=mesh,
        in_specs=(
            P("dp", "tensor"),
            P(None, "tensor"),
            P("tensor"),
            P("tensor", None),
            P(),
            P("dp", None),
            P("dp"),
            P(),
            P(),
        ),
        out_specs=(P(("dp", "tensor"), None), P(("dp", "tensor"), None)),
        check_vma=False,
    )
```

profile of v0, /device:TPU:1, one launch (start us, length us, event | category | flops | bytes accessed | tf_op | source)
XLA Modules:
  0.0 1826.9 jit_solution(6470894475168876882)
XLA Ops:
  7.2 15.4 all-gather
  28.2 57.7 %all-reduce.2.cloned.1.call-done = f32[64,1152]{1,0:T(8,128)} async-done(((f32[64,1152]{1,0:T(8,128)}), f32[64,1152]{1,0:T(8,128)}) %all-reduce.2.cloned.1.call-update) | async-done | bytes 294928 | tf_op jit(solution)/shard_map/psum | solution.py:94
  87.9 1706.4 %while.20 = (s32[]{:T(128)}, bf16[16,1152]{1,0:T(8,128)(2,1)S(1)}, f32[16,1152]{1,0:T(8,128)S(1)}, f32[64,1152]{1,0:T(8,128)S(1)}, f32[]{:T(128)}, /*index=5*/s3...) while((s32[]{:T(128)}, bf16[16,1152]{1,0:T(8,128)(2,1)S(1)}, ...), condition=%wide.region_6.7_spmd.clone, body=%wide.region_5.6_spmd.clone.sunk | while | flops 7256098 | bytes 1628964 | solution.py:132
  87.9 5.6 collective-permute-start
  98.6 4.3 collective-permute-start
  116.1 4.0 collective-permute-done
  170.0 4.0 collective-permute-done
  183.5 4.0 collective-permute-done
  196.9 4.0 collective-permute-done
  237.4 4.0 collective-permute-done
  250.8 4.0 collective-permute-done
  264.3 4.0 collective-permute-done
  318.2 4.0 collective-permute-done
  331.7 4.0 collective-permute-done
  385.5 4.0 collective-permute-done
  399.0 4.0 collective-permute-done
  412.5 4.0 collective-permute-done
  452.9 4.0 collective-permute-done
  466.4 4.0 collective-permute-done
  479.9 4.0 collective-permute-done
  533.7 4.0 collective-permute-done
  547.2 4.0 collective-permute-done
  601.1 4.0 collective-permute-done
  614.6 4.0 collective-permute-done
  668.5 4.0 collective-permute-done
  681.9 4.0 collective-permute-done
  695.4 4.0 collective-permute-done
  749.3 4.0 collective-permute-done
  762.8 4.0 collective-permute-done
  816.7 4.0 collective-permute-done
  830.1 4.0 collective-permute-done
  884.0 4.0 collective-permute-done
  897.5 4.0 collective-permute-done
  911.0 4.0 collective-permute-done
  964.8 4.0 collective-permute-done
  978.3 4.0 collective-permute-done
  1032.2 4.0 collective-permute-done
  1045.7 4.0 collective-permute-done
  1099.6 4.0 collective-permute-done
  1113.0 4.0 collective-permute-done
  1126.5 4.0 collective-permute-done
  1180.4 4.0 collective-permute-done
  1193.9 4.0 collective-permute-done
  1247.8 4.0 collective-permute-done
  1261.2 4.0 collective-permute-done
  1315.1 4.0 collective-permute-done
  1328.6 4.0 collective-permute-done
  1342.1 4.0 collective-permute-done
  1396.0 4.0 collective-permute-done
  1409.4 4.0 collective-permute-done
  1463.3 4.0 collective-permute-done
  1476.8 4.0 collective-permute-done
  1530.7 4.0 collective-permute-done
  1544.2 4.0 collective-permute-done
  1557.6 4.0 collective-permute-done
  1611.5 4.0 collective-permute-done
  1625.0 4.0 collective-permute-done
  1678.9 4.0 collective-permute-done
  1692.3 4.0 collective-permute-done
  1746.2 4.0 collective-permute-done
  1759.7 4.0 collective-permute-done
  1773.2 4.0 collective-permute-done
  1797.5 8.0 collective-permute-done.2
  1805.5 13.9 reduce-scatter.2.cloned.1.call-done
  (1117 shorter events, 1467.3 us)
Async XLA Ops:
  7.2 78.7 %all-reduce.2.cloned.1.call-start = ((), (), s32[]{:S(2)}) async-start(), calls=%async_computation.1 | async-start | bytes 589824 | tf_op jit(solution)/shard_map/psum | solution.py:94
  26.6 1792.9 %reduce-scatter.2.cloned.1.call-start = ((), (), s32[]{:S(2)}) async-start(), calls=%async_computation.2 | async-start | bytes 368640 | tf_op jit(solution)/shard_map/reduce_scatter | solution.py:146
  127.4 9.9 collective-permute-start.1
  140.8 9.9 collective-permute-start.1
  167.8 9.9 collective-permute-start.1
  181.2 9.9 collective-permute-start.1
  194.7 9.9 collective-permute-start.1
  221.7 9.9 collective-permute-start.1
  235.1 9.9 collective-permute-start.1
  248.6 9.9 collective-permute-start.1
  275.5 9.9 collective-permute-start.1
  289.0 9.9 collective-permute-start.1
  329.4 9.9 collective-permute-start.1
  342.9 9.9 collective-permute-start.1
  383.3 9.9 collective-permute-start.1
  396.8 9.9 collective-permute-start.1
  423.7 9.9 collective-permute-start.1
  437.2 9.9 collective-permute-start.1
  450.7 9.9 collective-permute-start.1
  477.6 9.9 collective-permute-start.1
  491.1 9.9 collective-permute-start.1
  504.6 9.9 collective-permute-start.1
  531.5 9.9 collective-permute-start.1
  545.0 9.9 collective-permute-start.1
  585.4 9.9 collective-permute-start.1
  598.9 9.9 collective-permute-start.1
  639.3 9.9 collective-permute-start.1
  652.8 9.9 collective-permute-start.1
  679.7 9.9 collective-permute-start.1
  693.2 9.9 collective-permute-start.1
  706.7 9.9 collective-permute-start.1
  733.6 9.9 collective-permute-start.1
  747.1 9.9 collective-permute-start.1
  760.5 9.9 collective-permute-start.1
  787.5 9.9 collective-permute-start.1
  801.0 9.9 collective-permute-start.1
  841.4 9.9 collective-permute-start.1
  854.8 9.9 collective-permute-start.1
  895.3 9.9 collective-permute-start.1
  908.7 9.9 collective-permute-start.1
  935.7 9.9 collective-permute-start.1
  949.1 9.9 collective-permute-start.1
  962.6 9.9 collective-permute-start.1
  989.6 9.9 collective-permute-start.1
  1003.0 9.9 collective-permute-start.1
  1016.5 9.9 collective-permute-start.1
  1043.5 9.9 collective-permute-start.1
  1056.9 9.9 collective-permute-start.1
  1097.3 9.9 collective-permute-start.1
  1110.8 9.9 collective-permute-start.1
  1151.2 9.9 collective-permute-start.1
  1164.7 9.9 collective-permute-start.1
  1191.6 9.9 collective-permute-start.1
  1205.1 9.9 collective-permute-start.1
  1218.6 9.9 collective-permute-start.1
  1245.5 9.9 collective-permute-start.1
  1259.0 9.9 collective-permute-start.1
  1272.5 9.9 collective-permute-start.1
  1299.4 9.9 collective-permute-start.1
  1312.9 9.9 collective-permute-start.1
  1353.3 9.9 collective-permute-start.1
  1366.8 9.9 collective-permute-start.1
  1407.2 9.9 collective-permute-start.1
  1420.7 9.9 collective-permute-start.1
  (197 other events, 2034.8 us)
Sparse Core Ops, SparseCore 0:
  26.7 59.1 all-reduce.1
  1795.6 23.7 reduce-scatter.1
where the time goes:
time: 1850 us; the launch traced here: 1830 us
  waiting for transfers between devices  1040 us (56%)
  starting transfers between devices  494 us (27%)
  matrix products  245 us (13%)
    ppermute x255, waiting for transfers between devices, from_behind(): lax.ppermute(shard, axis, [(i, (i + by) % length) for i in range(length)])  970 us
    ppermute x255, starting transfers between devices, from_behind(): lax.ppermute(shard, axis, [(i, (i + by) % length) for i in range(length)])  494 us
    dot_general x128, matrix products, couple_losses(): lax.dot_general(layer_group, picture_direction, (((1,), (1,)), ((), ())),...  187 us
    psum x1, waiting for transfers between devices, shards(): lax.psum(jnp.dot(hidden, second_dense_matrix, preferred_element_type=jnp....  57.7 us
    dot_general x128, matrix products, couple_losses(): lax.dot_general(sigmoid_coefficients, layer_group, (((0,), (0,)), ((), ()...  37.1 us
  transfers between devices with their start and end apart: 257, of which 255 were waited for; matrix products, arithmetic and copies ran while one was open for 13% of the time, Pallas kernels for 0%

commit v1 on v0

v1 whole, which is shorter than its diff:
```python
import jax
import jax.numpy as jnp
from jax import lax
from jax.sharding import Mesh, PartitionSpec as P

EPSILON = 1e-06
ROWS = ("yl", "z", "x", "core")
BF16 = jnp.bfloat16
F32 = jnp.float32


def spread(block, axes):
    count = lax.axis_size(axes)
    return lax.all_to_all(jnp.broadcast_to(block[None], (count,) + block.shape), axes, 0, 0)


def layer_norm(values):
    widened = values.astype(F32)
    centred = widened - jnp.mean(widened, axis=-1, keepdims=True)
    variance = jnp.mean(centred * centred, axis=-1, keepdims=True)
    return (centred * lax.rsqrt(variance + EPSILON)).astype(BF16)


def unit_rows(values):
    squared = jnp.sum(values * values, axis=-1, keepdims=True)
    return (values * lax.rsqrt(squared + EPSILON)).astype(BF16)


def shards(tokens, w1, b1, w2, b2, pictures, matching, sharpness, offset):
    scale, shift = sharpness[0], offset[0]
    t = lax.axis_index("t")
    x, core = lax.axis_index("x"), lax.axis_index("core")
    width = pictures.shape[1]

    image_unit = unit_rows(pictures.astype(F32))
    lane = lax.broadcasted_iota(jnp.int32, (matching.shape[0], 128), 1)
    digits = jnp.where(lane == 0, matching[:, None] // 128, jnp.where(lane == 1, matching[:, None] % 128, 0))
    packed = jnp.concatenate([image_unit, digits.astype(BF16)], axis=1)
    images = lax.all_gather(packed, ("x", "core"), axis=0, tiled=True)

    gathered = spread(tokens, "t")
    gathered = jnp.transpose(gathered, (1, 0, 2)).reshape(tokens.shape[0], width)
    normed = layer_norm(gathered)
    hidden = jax.nn.gelu(
        jnp.dot(normed, w1, preferred_element_type=F32) + b1, approximate=True
    ).astype(BF16)
    partial = jnp.dot(hidden, w2, preferred_element_type=F32)
    own = tokens.shape[0] // lax.axis_size("t")
    partial = lax.all_to_all(partial.reshape(-1, own, width), "t", 0, 0)
    residual = lax.dynamic_slice_in_dim(gathered, t * own, own, 0).astype(F32)
    text_own = unit_rows(residual + jnp.sum(partial, axis=0) + b2)
    text = spread(text_own, ("yl", "z"))
    groups = text.shape[0]
    text = text.reshape(groups * own, width)

    image = images[:, :width]
    position = images[:, width].astype(F32) * 128.0 + images[:, width + 1].astype(F32)
    block = lax.axis_size("core") * lax.axis_size("x") * tokens.shape[0]
    first = (x * lax.axis_size("core") + core) * tokens.shape[0] + t * own
    number = jnp.arange(groups * own, dtype=jnp.int32)
    ids = (number // own) * block + first + number % own
    matched = position.astype(jnp.int32)[:, None] == ids[None, :]
    scores = scale * lax.dot_general(
        image, text, (((1,), (1,)), ((), ())), preferred_element_type=F32
    ) + shift
    sign = jnp.where(matched, 1.0, -1.0).astype(F32)
    weights = (-scale * sign * jax.nn.sigmoid(-sign * scores)).astype(BF16)
    text_share = lax.dot_general(weights, image, (((0,), (0,)), ((), ())), preferred_element_type=F32)
    image_share = jnp.dot(weights, text, preferred_element_type=F32)

    text_parts = lax.all_to_all(
        text_share.astype(BF16).reshape(groups, own, width), ("yl", "z"), 0, 0
    )
    text_grad = jnp.sum(text_parts.astype(F32), axis=0)
    sized = image_share.reshape(lax.axis_size("x"), lax.axis_size("core"), lax.axis_size("t"), own, width)
    away = lax.dynamic_index_in_dim(sized, 1 - core, 1, keepdims=False).astype(BF16)
    mine = lax.dynamic_index_in_dim(sized, core, 1, keepdims=False)
    came = lax.ppermute(away, "core", [(0, 1), (1, 0)])
    pair = (mine + came.astype(F32)).astype(BF16).reshape(-1, own, width)
    image_parts = lax.all_to_all(pair, ("x", "t"), 0, 0)
    image_grad = jnp.sum(image_parts.astype(F32), axis=0)
    return text_grad, image_grad


def solution(mesh):
    fine = Mesh(mesh.devices.reshape(2, 8, 4, 2, 4), ROWS + ("t",))
    return jax.shard_map(
        shards,
        mesh=fine,
        in_specs=(
            P(ROWS, "t"),
            P(None, "t"),
            P("t"),
            P("t", None),
            P(),
            P(ROWS, None),
            P(ROWS),
            P(),
            P(),
        ),
        out_specs=(P(ROWS + ("t",), None), P(ROWS + ("t",), None)),
        check_vma=False,
    )
```

time: 1850 us -> 127 us (0.07)
  the two profiles are of different devices: /device:TPU:1 before, /device:TPU:72 now
where the time goes in v1:
time: 127 us
  waiting for transfers between devices  55.3 us (44%)
  starting transfers between devices  35.3 us (28%)
  between operations  15.5 us (12%)
  other arithmetic  7.75 us (6%)
  matrix products  6.97 us (5%)
  local copies, waits for them, and re-layouts  5.65 us (4%)
    all_to_all x1, waiting for transfers between devices, shards(): image_parts = lax.all_to_all(pair, ('x', 't'), 0, 0)  18.6 us
    all_to_all x2, starting transfers between devices, spread(): lax.all_to_all(jnp.broadcast_to(block[None], (count,) + block.shape), axe...  17.2 us
    all_to_all x2, waiting for transfers between devices, spread(): lax.all_to_all(jnp.broadcast_to(block[None], (count,) + block.shape), axe...  16.3 us
    all_to_all x1, waiting for transfers between devices, shards(): partial = lax.all_to_all(partial.reshape(-1, own, width), 't', 0, 0)  10.6 us
    all_to_all x1, starting transfers between devices, shards(): image_parts = lax.all_to_all(pair, ('x', 't'), 0, 0)  7.89 us
    all_to_all x1, waiting for transfers between devices, shards(): lax.all_to_all(text_share.astype(BF16).reshape(groups, own, width), ('yl'...  7.87 us
    all_to_all x1, starting transfers between devices, shards(): lax.all_to_all(text_share.astype(BF16).reshape(groups, own, width), ('yl'...  4.86 us
    all_to_all x1, starting transfers between devices, shards(): partial = lax.all_to_all(partial.reshape(-1, own, width), 't', 0, 0)  3.45 us
  transfers between devices with their start and end apart: 7, of which 6 were waited for; matrix products, arithmetic and copies ran while one was open for 10% of the time, Pallas kernels for 0%

profile of v1, /device:TPU:72, one launch (start us, length us, event | category | flops | bytes accessed | tf_op | source)
XLA Modules:
  0.0 126.5 jit_solution(11122084653395903273)
XLA Ops:
  7.2 0.0 copy-start
  7.2 1.6 %broadcast_in_dim.32 = bf16[4,64,288]{2,1,0:T(8,128)(2,1)} broadcast(bf16[64,288]{1,0:T(8,128)(2,1)} %param.9), dimensions={1,2} | broadcast | bytes 184320 | tf_op jit(solution)/shard_map/broadcast_in_dim | solution.py:14
  8.8 0.0 copy-start.4
  8.8 6.3 %all-to-all-start = ((bf16[4,64,288]{2,1,0:T(8,128)(2,1)}), bf16[4,64,288]{2,1,0:T(8,128)(2,1)S(1)}, u32[]{:S(2)}, u32[]{:S(2)}) async-start(bf16[4,64,288]{2,1,0:T(8,128)(2,1)} %broadcast_in_dim.32), calls=%async_computation | async-start | bytes 393216 | tf_op jit(solution)/shard_map/all_to_all | solution.py:14
  15.1 0.0 all-gather.2.cloned.1.call-start
  15.2 1.0 fusion.14
  16.2 0.7 and_select_fusion.3
  16.9 1.0 fusion.15
  17.9 0.1 select_convert_fusion
  18.0 0.7 pad_maximum_fusion
  18.7 0.0 all-gather.2.cloned.1.call-update
  18.7 6.2 %all-to-all-done = bf16[4,64,288]{2,1,0:T(8,128)(2,1)S(1)} async-done(((bf16[4,64,288]{2,1,0:T(8,128)(2,1)}), bf16[4,64,288]{2,1,0:T(8,128)(2,1)S(1)}, u32[]{:S(2)}, u32[]{:S(2)}) %all-to-all-start) | async-done | bytes 147488 | tf_op jit(solution)/shard_map/all_to_all | solution.py:14
  24.9 0.1 convert_reduce_fusion.2
  25.1 0.2 fusion.13
  25.3 0.2 copy.16
  25.5 0.2 reshape.104
  25.6 0.0 copy-done
  25.7 0.0 copy-done.4
  25.7 0.0 copy-start.3
  25.7 3.1 %fusion.24 = f32[64,1152]{1,0:T(8,128)} fusion(bf16[768,1152]{1,0:T(8,128)(2,1)S(1)} %copy-done, bf16[1152,768]{1,0:T(8,128)(2,1)} %param.10, bf16[64,1152]{1,0:T(8,128)(2,1)S(1)} %reshape.104, f32[64]{0:T(128)S(1)} %add_rsqrt_fusion.1, f32[64]{0:T(128)S(1)} %broadcast_multiply_fusion, f32[768]{0:T(1024)S(1)} %copy-done.4), kind=kOutput, calls=%fused_computation.39 | convolution fusion | flops 227278848 | bytes 3984896 | tf_op jit(solution)/shard_map/dot_general | solution.py:47
  28.8 3.5 %all-to-all-start.1 = ((f32[4,16,1152]{2,1,0:T(8,128)}), f32[4,16,1152]{2,1,0:T(8,128)S(1)}, u32[]{:S(2)}, u32[]{:S(2)}) async-start(f32[4,16,1152]{2,1,0:T(8,128)} %bitcast.3), calls=%async_computation.1 | async-start | bytes 589824 | tf_op jit(solution)/shard_map/all_to_all | solution.py:49
  32.3 10.6 %all-to-all-done.1 = f32[4,16,1152]{2,1,0:T(8,128)S(1)} async-done(((f32[4,16,1152]{2,1,0:T(8,128)}), f32[4,16,1152]{2,1,0:T(8,128)S(1)}, u32[]{:S(2)}, u32[]{:S(2)}) %all-to-all-start.1) | async-done | bytes 294944 | tf_op jit(solution)/shard_map/all_to_all | solution.py:49
  42.9 0.0 copy-done.3
  42.9 0.1 multiply_reduce_fusion
  43.0 0.1 multiply_convert_fusion.3
  43.1 0.9 broadcast_in_dim.33
  44.0 10.9 %all-to-all-start.2 = ((bf16[16,16,1152]{2,1,0:T(8,128)(2,1)}), bf16[16,16,1152]{2,1,0:T(8,128)(2,1)S(1)}, u32[]{:S(2)}, u32[]{:S(2)}) async-start(bf16[16,16,1152]{2,1,0:T(8,128)(2,1)} %broadcast_in_dim.33), calls=%async_computation.2 | async-start | bytes 1179648 | tf_op jit(solution)/shard_map/all_to_all | solution.py:14
  56.2 0.0 all-gather.2.cloned.1.call-done
  56.2 1.1 fusion.43
  57.3 0.1 copy.18
  57.4 0.1 copy.19
  57.6 10.0 %all-to-all-done.2 = bf16[16,16,1152]{2,1,0:T(8,128)(2,1)S(1)} async-done(((bf16[16,16,1152]{2,1,0:T(8,128)(2,1)}), bf16[16,16,1152]{2,1,0:T(8,128)(2,1)S(1)}, u32[]{:S(2)}, u32[]{:S(2)}) %all-to-all-start.2) | async-done | bytes 589856 | tf_op jit(solution)/shard_map/all_to_all | solution.py:14
  67.6 0.0 copy-start.2
  67.6 2.0 %fusion.7 = bf16[512,256]{1,0:T(8,128)(2,1)S(1)} fusion(bf16[256,1152]{1,0:T(8,128)(2,1)S(1)} %bitcast.31, bf16[512,1280]{1,0:T(8,128)(2,1)} %all-gather.2.cloned.1.call-done, f32[]{:T(128)} %bitcast.29, f32[]{:T(128)} %bitcast.28, s32[256]{0:T(256)S(1)} %fusion.36, f32[]{:T(128)S(6)} %neg.9, s32[512]{0:T(512)S(1)} %bitcast.34), kind=kOutput, calls=%fused_computation.9 | convolution fusion | flops 303562752 | bytes 2035716 | tf_op jit(solution)/shard_map/dot_general | solution.py:63
  69.6 0.0 copy-done.2
  69.6 1.3 %convolution_convert_fusion = bf16[256,1152]{1,0:T(8,128)(2,1)} fusion(bf16[512,256]{1,0:T(8,128)(2,1)S(1)} %fusion.7, bf16[512,1280]{1,0:T(8,128)(2,1)S(1)} %copy-done.2), kind=kOutput, calls=%fused_computation | convolution fusion | flops 302284800 | bytes 2031616 | tf_op jit(solution)/shard_map/dot_general | solution.py:68
  70.9 4.9 %all-to-all-start.3 = ((bf16[16,16,1152]{2,1,0:T(8,128)(2,1)}), bf16[16,16,1152]{2,1,0:T(8,128)(2,1)S(1)}, u32[]{:S(2)}, u32[]{:S(2)}) async-start(bf16[16,16,1152]{2,1,0:T(8,128)(2,1)} %bitcast.6), calls=%async_computation.3 | async-start | bytes 1179648 | tf_op jit(solution)/shard_map/all_to_all | solution.py:71
  75.8 0.5 fusion.44
  76.3 0.0 copy-start.1
  76.3 1.4 %copy-done.1 = f32[4,2,4,16,1152]{4,3,2,1,0:T(8,128)} copy-done((f32[4,2,4,16,1152]{4,3,2,1,0:T(8,128)}, f32[4,2,4,16,1152]{4,3,2,1,0:T(8,128)S(1)}, u32[]{:S(2)}) %copy-start.1) | copy-done | bytes 2359320
  77.7 0.1 fusion.11
  77.8 1.9 %collective-permute-start = (bf16[4,4,16,1152]{3,2,1,0:T(8,128)(2,1)S(1)}, bf16[4,4,16,1152]{3,2,1,0:T(8,128)(2,1)S(1)}, u32[]{:S(2)}, u32[]{:S(2)}) collective-permute-start(bf16[4,4,16,1152]{3,2,1,0:T(8,128)(2,1)S(1)} %fusion.11), channel_id=1, source_target_pairs={{0,4},{4,0},{1,5},{5,1},{2,6},{6,2},{3,7},{7,3},{8,12},{12,8},{9,1... | collective-permute-start | bytes 1769480 | tf_op jit(solution)/shard_map/ppermute | solution.py:78
  79.7 2.0 %collective-permute-done = bf16[4,4,16,1152]{3,2,1,0:T(8,128)(2,1)S(1)} collective-permute-done((bf16[4,4,16,1152]{3,2,1,0:T(8,128)(2,1)S(1)}, bf16[4,4,16,1152]{3,2,1,0:T(8,128)(2,1)S(1)}, u32[]{:S(2)}, u32[]{:S(2)}) %collective-permute-start) | collective-permute-done | bytes 589856 | tf_op jit(solution)/shard_map/ppermute | solution.py:78
  81.7 2.2 %fusion.8 = bf16[4,4,16,1152]{3,2,1,0:T(8,128)(2,1)} fusion(bf16[4,4,16,1152]{3,2,1,0:T(8,128)(2,1)S(1)} %collective-permute-done, f32[4,2,4,16,1152]{4,3,2,1,0:T(8,128)} %copy-done.1, s32[]{:T(128)S(6)} %select_n.63), kind=kLoop, calls=%fused_computation.11 | loop fusion | flops 884736 | bytes 2359300 | tf_op jit(solution)/shard_map/convert_element_type | solution.py:79
  83.9 7.9 %all-to-all-done.3 = bf16[16,16,1152]{2,1,0:T(8,128)(2,1)S(1)} async-done(((bf16[16,16,1152]{2,1,0:T(8,128)(2,1)}), bf16[16,16,1152]{2,1,0:T(8,128)(2,1)S(1)}, u32[]{:S(2)}, u32[]{:S(2)}) %all-to-all-start.3) | async-done | bytes 589856 | tf_op jit(solution)/shard_map/all_to_all | solution.py:71
  91.8 7.9 %all-to-all-start.4 = ((bf16[16,16,1152]{2,1,0:T(8,128)(2,1)}), bf16[16,16,1152]{2,1,0:T(8,128)(2,1)S(1)}, u32[]{:S(2)}, u32[]{:S(2)}) async-start(bf16[16,16,1152]{2,1,0:T(8,128)(2,1)} %bitcast.12), calls=%async_computation.4 | async-start | bytes 1179648 | tf_op jit(solution)/shard_map/all_to_all | solution.py:80
  99.7 0.7 convert_reduce_fusion.1
  100.4 18.6 %all-to-all-done.4 = bf16[16,16,1152]{2,1,0:T(8,128)(2,1)S(1)} async-done(((bf16[16,16,1152]{2,1,0:T(8,128)(2,1)}), bf16[16,16,1152]{2,1,0:T(8,128)(2,1)S(1)}, u32[]{:S(2)}, u32[]{:S(2)}) %all-to-all-start.4) | async-done | bytes 589856 | tf_op jit(solution)/shard_map/all_to_all | solution.py:80
  119.0 0.7 convert_reduce_fusion
  (8 shorter events, 0.1 us)
Async XLA Ops:
  7.2 18.5 %copy-start = (bf16[768,1152]{1,0:T(8,128)(2,1)S(1)}, bf16[768,1152]{1,0:T(8,128)(2,1)}, u32[]{:S(2)}) copy-start(bf16[768,1152]{1,0:T(8,128)(2,1)} %param.12) | copy-start | bytes 5308420
  8.8 16.8 %copy-start.4 = (f32[768]{0:T(1024)S(1)}, f32[768]{0:T(1024)}, u32[]{:S(2)}) copy-start(f32[768]{0:T(1024)} %param.11) | copy-start | bytes 9220
  8.8 16.1 %all-to-all-start = ((bf16[4,64,288]{2,1,0:T(8,128)(2,1)}), bf16[4,64,288]{2,1,0:T(8,128)(2,1)S(1)}, u32[]{:S(2)}, u32[]{:S(2)}) async-start(bf16[4,64,288]{2,1,0:T(8,128)(2,1)} %broadcast_in_dim.32), calls=%async_computation | async-start | bytes 393216 | tf_op jit(solution)/shard_map/all_to_all | solution.py:14
  15.1 41.1 %all-gather.2.cloned.1.call-start = ((), (), s32[]{:S(2)}) async-start(), calls=%async_computation.5 | async-start | bytes 1474560 | tf_op jit(solution)/shard_map/all_gather | solution.py:39
  25.7 17.2 %copy-start.3 = (f32[1152]{0:T(1024)S(1)}, f32[1152]{0:T(1024)}, u32[]{:S(2)}) copy-start(f32[1152]{0:T(1024)} %param.13) | copy-start | bytes 13828
  28.8 14.1 %all-to-all-start.1 = ((f32[4,16,1152]{2,1,0:T(8,128)}), f32[4,16,1152]{2,1,0:T(8,128)S(1)}, u32[]{:S(2)}, u32[]{:S(2)}) async-start(f32[4,16,1152]{2,1,0:T(8,128)} %bitcast.3), calls=%async_computation.1 | async-start | bytes 589824 | tf_op jit(solution)/shard_map/all_to_all | solution.py:49
  44.0 23.6 %all-to-all-start.2 = ((bf16[16,16,1152]{2,1,0:T(8,128)(2,1)}), bf16[16,16,1152]{2,1,0:T(8,128)(2,1)S(1)}, u32[]{:S(2)}, u32[]{:S(2)}) async-start(bf16[16,16,1152]{2,1,0:T(8,128)(2,1)} %broadcast_in_dim.33), calls=%async_computation.2 | async-start | bytes 1179648 | tf_op jit(solution)/shard_map/all_to_all | solution.py:14
  67.6 2.0 %copy-start.2 = (bf16[512,1280]{1,0:T(8,128)(2,1)S(1)}, bf16[512,1280]{1,0:T(8,128)(2,1)}, u32[]{:S(2)}) copy-start(bf16[512,1280]{1,0:T(8,128)(2,1)} %all-gather.2.cloned.1.call-done) | copy-start | bytes 3932164
  70.9 20.8 %all-to-all-start.3 = ((bf16[16,16,1152]{2,1,0:T(8,128)(2,1)}), bf16[16,16,1152]{2,1,0:T(8,128)(2,1)S(1)}, u32[]{:S(2)}, u32[]{:S(2)}) async-start(bf16[16,16,1152]{2,1,0:T(8,128)(2,1)} %bitcast.6), calls=%async_computation.3 | async-start | bytes 1179648 | tf_op jit(solution)/shard_map/all_to_all | solution.py:71
  76.3 1.4 %copy-start.1 = (f32[4,2,4,16,1152]{4,3,2,1,0:T(8,128)}, f32[4,2,4,16,1152]{4,3,2,1,0:T(8,128)S(1)}, u32[]{:S(2)}) copy-start(f32[4,2,4,16,1152]{4,3,2,1,0:T(8,128)S(1)} %fusion.44) | copy-start | bytes 7077892
  77.8 3.9 %collective-permute-start = (bf16[4,4,16,1152]{3,2,1,0:T(8,128)(2,1)S(1)}, bf16[4,4,16,1152]{3,2,1,0:T(8,128)(2,1)S(1)}, u32[]{:S(2)}, u32[]{:S(2)}) collective-permute-start(bf16[4,4,16,1152]{3,2,1,0:T(8,128)(2,1)S(1)} %fusion.11), channel_id=1, source_target_pairs={{0,4},{4,0},{1,5},{5,1},{2,6},{6,2},{3,7},{7,3},{8,12},{12,8},{9,1... | collective-permute-start | bytes 1769480 | tf_op jit(solution)/shard_map/ppermute | solution.py:78
  91.8 27.2 %all-to-all-start.4 = ((bf16[16,16,1152]{2,1,0:T(8,128)(2,1)}), bf16[16,16,1152]{2,1,0:T(8,128)(2,1)S(1)}, u32[]{:S(2)}, u32[]{:S(2)}) async-start(bf16[16,16,1152]{2,1,0:T(8,128)(2,1)} %bitcast.12), calls=%async_computation.4 | async-start | bytes 1179648 | tf_op jit(solution)/shard_map/all_to_all | solution.py:80
Sparse Core Ops, SparseCore 0:
  18.8 34.2 all-gather.1

commit v2 on v1

v2 whole, which is shorter than its diff:
```python
import functools

import jax
import jax.numpy as jnp
from jax import lax
from jax.experimental import pallas as pl
from jax.experimental.pallas import tpu as pltpu
from jax.sharding import Mesh, PartitionSpec as P

EPSILON = 1e-06
ROWS = ("yl", "z", "x", "core")
ALL = ROWS + ("t",)
SIZES = dict(yl=2, z=8, x=4, core=2, t=4)
BF16 = jnp.bfloat16
F32 = jnp.float32
LANES = 128
VMEM = pl.BlockSpec(memory_space=pltpu.VMEM)
SMEM = pl.BlockSpec(memory_space=pltpu.SMEM)


def nt(a, b):
    return lax.dot_general(a, b, (((1,), (1,)), ((), ())), preferred_element_type=F32)


def nn(a, b):
    return jnp.dot(a, b, preferred_element_type=F32)


def call(kernel, outs, operands, scalars=0, flops=0):
    return pl.pallas_call(
        kernel,
        out_shape=outs,
        in_specs=[SMEM] * scalars + [VMEM] * (len(operands) - scalars),
        out_specs=jax.tree.map(lambda _: VMEM, outs),
        compiler_params=pltpu.CompilerParams(vmem_limit_bytes=40 * 2**20),
        cost_estimate=pl.CostEstimate(flops=flops, bytes_accessed=100_000, transcendentals=0),
    )(*operands)


def spread(block, axes):
    count = lax.axis_size(axes)
    return lax.all_to_all(jnp.broadcast_to(block[None], (count,) + block.shape), axes, 0, 0)


def swap_cores(block):
    return lax.ppermute(block, "core", [(0, 1), (1, 0)])


def from_behind(block, by):
    length = lax.axis_size("x")
    return lax.ppermute(block, "x", [(i, (i + by) % length) for i in range(length)])


def grad_groups():
    yl, z, x, core, t = (SIZES[a] for a in ALL)

    def flat(i, j, k, c, m):
        return (((i * z + j) * x + k) * core + c) * t + m

    text = [[flat(i, j, k, 0, m) for i in range(yl) for j in range(z)] for k in range(x) for m in range(t)]
    image = [[flat(i, j, k, 1, m) for k in range(x) for m in range(t)] for i in range(yl) for j in range(z)]
    return text + image


def unit(values):
    squared = jnp.sum(values * values, axis=-1, keepdims=True)
    return (values * lax.rsqrt(squared + EPSILON)).astype(BF16)


def pack_kernel(pictures, position, packed):
    width = pictures.shape[1]
    packed[:, :width] = unit(pictures[...].astype(F32))
    where = position[...]
    lane = lax.broadcasted_iota(jnp.int32, (where.shape[0], LANES), 1)
    digits = jnp.where(lane == 0, where // LANES, jnp.where(lane == 1, where % LANES, 0))
    packed[:, width:] = digits.astype(F32).astype(BF16)


def ffn_kernel(first, gathered, w1, b1, w2, b2, partial):
    parts = [gathered[k].astype(F32) for k in range(gathered.shape[0])]
    tokens = jnp.concatenate(parts, axis=1)
    centred = tokens - jnp.mean(tokens, axis=-1, keepdims=True)
    variance = jnp.mean(centred * centred, axis=-1, keepdims=True)
    normed = (centred * lax.rsqrt(variance + EPSILON)).astype(BF16)
    hidden = jax.nn.gelu(nn(normed, w1[...]) + b1[...], approximate=True).astype(BF16)
    branch = nn(hidden, w2[...])
    kept = jnp.where(first[0] == 0, tokens + b2[...], 0.0)
    partial[...] = (branch + kept).reshape(partial.shape)


def text_kernel(parts, copies):
    total = parts[0]
    for k in range(1, parts.shape[0]):
        total = total + parts[k]
    row = unit(total)
    for k in range(copies.shape[0]):
        copies[k] = row


def pair_kernel(place, numbers, text_own, text_other, image_own, image_other, out):
    groups, _, own, width = out.shape
    x, core, t = place[0], place[1], place[2]
    scale, shift = numbers[0], numbers[1]
    ring, tensor = SIZES["x"], SIZES["t"]
    block = tensor * own
    lane = lax.broadcasted_iota(jnp.int32, (8, LANES), 1)
    digit = jnp.where(lane == 0, float(LANES), jnp.where(lane == 1, 1.0, 0.0)).astype(BF16)

    def ids(shape, dim, which):
        row = lax.broadcasted_iota(jnp.int32, shape, dim)
        first = (x * 2 + which) * block + t * own
        return ((row // own) * (ring * 2 * block) + first + row % own).astype(F32)

    def weights(a, b, match):
        scores = scale * nt(a, b) + shift
        score = jnp.where(match, -scores, scores)
        size = jnp.where(match, -scale, scale)
        return (size / (1.0 + jnp.exp(-score))).astype(BF16)

    texts = ((text_own, core), (text_other, 1 - core))
    images = ((image_own, core), (image_other, 1 - core))
    many = groups * own

    @pl.when(core == 0)
    def _():
        for which, (text, from_core) in enumerate(texts):
            a = text[...].reshape(many, width)
            total = None
            for image, _ in images:
                b = image[:, :width]
                position = nt(digit, image[:, width:])[:1]
                match = ids((many, 1), 0, from_core) == position
                part = nn(weights(a, b, match), b)
                total = part if total is None else total + part
            out[:, which] = total.astype(BF16).reshape(groups, own, width)

    @pl.when(core == 1)
    def _():
        for which, (image, from_core) in enumerate(images):
            a = image[:, :width]
            position = nt(image[:, width:], digit)[:, :1]
            total = None
            for text, text_core in texts:
                b = text[...].reshape(many, width)
                match = position == ids((1, many), 1, text_core)
                part = nn(weights(a, b, match), b)
                total = part if total is None else total + part
            total = total.astype(BF16)
            for k in range(ring):
                at = lax.rem(x + ring - k, ring)
                rows = total[k * block : (k + 1) * block].reshape(tensor, own, width)
                out[pl.ds(at * tensor, tensor), 1 - which] = rows


def sum_kernel(core, parts, keep, send):
    def total(which):
        value = parts[0, which].astype(F32)
        for k in range(1, parts.shape[0]):
            value = value + parts[k, which].astype(F32)
        return value

    first, second = total(0), total(1)
    keep[...] = jnp.where(core[0] == 0, first, second)
    send[...] = jnp.where(core[0] == 0, second, first)


def shards(tokens, w1, b1, w2, b2, pictures, matching, sharpness, offset):
    x, core, t = (lax.axis_index(a).astype(jnp.int32) for a in ("x", "core", "t"))
    place = jnp.stack([x, core, t])
    rows, width = pictures.shape
    tensor, ring = lax.axis_size("t"), lax.axis_size("x")
    own = rows // tensor
    groups = lax.axis_size(("yl", "z"))

    gathered = spread(tokens, "t")
    packed = call(
        pack_kernel,
        jax.ShapeDtypeStruct((rows, width + LANES), BF16),
        (pictures, matching[:, None]),
    )
    moved = [from_behind(packed, k) for k in range(1, ring)]
    partial = call(
        ffn_kernel,
        jax.ShapeDtypeStruct((tensor, own, width), F32),
        (t[None], gathered, w1, b1[None], w2, b2[None]),
        scalars=1,
    )
    partial, packed, *moved = lax.optimization_barrier((partial, packed, *moved))
    parts = lax.all_to_all(partial, "t", 0, 0)
    image_own = jnp.concatenate([packed] + moved, axis=0)
    image_other = swap_cores(image_own)
    parts, image_other = lax.optimization_barrier((parts, image_other))
    copies = call(text_kernel, jax.ShapeDtypeStruct((groups, own, width), BF16), (parts,))
    text_own = lax.all_to_all(copies, ("yl", "z"), 0, 0)
    text_other = swap_cores(text_own)
    numbers = jnp.concatenate([sharpness, offset])
    shares = call(
        pair_kernel,
        jax.ShapeDtypeStruct((groups, 2, own, width), BF16),
        (place, numbers, text_own, text_other, image_own, image_other),
        scalars=2,
        flops=1_200_000_000,
    )
    shares = lax.all_to_all(shares, ALL, 0, 0, axis_index_groups=grad_groups())
    half = jax.ShapeDtypeStruct((own, width), F32)
    keep, send = call(sum_kernel, (half, half), (core[None], shares), scalars=1)
    came = swap_cores(send)
    return jnp.where(core == 0, keep, came), jnp.where(core == 0, came, keep)


def solution(mesh):
    fine = Mesh(mesh.devices.reshape([SIZES[a] for a in ALL]), ALL)
    return jax.shard_map(
        shards,
        mesh=fine,
        in_specs=(
            P(ROWS, "t"),
            P(None, "t"),
            P("t"),
            P("t", None),
            P(),
            P(ROWS, None),
            P(ROWS),
            P(),
            P(),
        ),
        out_specs=(P(ALL, None), P(ALL, None)),
        check_vma=False,
    )
```

time: 127 us -> 116 us (0.913)
  the two profiles are of different devices: /device:TPU:72 before, /device:TPU:1 now
where the time goes in v2:
time: 116 us; the launch traced here: 115 us
  blocking collectives  70.2 us (61%)
  starting transfers between devices  29.2 us (25%)
  local copies, waits for them, and re-layouts  7.54 us (6%)
  Pallas kernels  4.01 us (3%)
  between operations  2.08 us (2%)
    all_to_all x1, blocking collectives, shards(): text_own = lax.all_to_all(copies, ('yl', 'z'), 0, 0)  26.8 us
    all_to_all x1, blocking collectives, shards(): shares = lax.all_to_all(shares, ALL, 0, 0, axis_index_groups=grad_groups())  26 us
    all_to_all x1, blocking collectives, shards(): parts = lax.all_to_all(partial, 't', 0, 0)  17.4 us
    ppermute x3, starting transfers between devices, swap_cores(): return lax.ppermute(block, 'core', [(0, 1), (1, 0)])  11 us
    ppermute x3, starting transfers between devices, from_behind(): lax.ppermute(block, 'x', [(i, (i + by) % length) for i in range(length)])  10.5 us
    all_to_all x1, starting transfers between devices, spread(): lax.all_to_all(jnp.broadcast_to(block[None], (count,) + block.shape), axe...  7.64 us
    pallas_call x5, Pallas kernels, call(): pl.pallas_call(kernel, out_shape=outs, in_specs=[SMEM] * scalars + [VMEM]...  4.01 us
    unnamed x9, local copies, waits for them, and re-layouts  3.9 us
  transfers between devices with their start and end apart: 7, of which 2 were waited for; matrix products, arithmetic and copies ran while one was open for 2% of the time, Pallas kernels for 1%

profile of v2, /device:TPU:1, one launch (start us, length us, event | category | flops | bytes accessed | tf_op | source)
XLA Modules:
  0.0 114.9 jit_solution(15371991951214405893)
XLA Ops:
  0.6 1.5 %broadcast_in_dim.20 = bf16[4,64,288]{2,1,0:T(8,128)(2,1)} broadcast(bf16[64,288]{1,0:T(8,128)(2,1)} %param.9), dimensions={1,2} | broadcast | bytes 184320 | tf_op jit(solution)/shard_map/broadcast_in_dim | solution.py:42
  2.1 7.6 %all-to-all-start = ((bf16[4,64,288]{2,1,0:T(8,128)(2,1)}), bf16[4,64,288]{2,1,0:T(8,128)(2,1)S(1)}, u32[]{:S(2)}, u32[]{:S(2)}) async-start(bf16[4,64,288]{2,1,0:T(8,128)(2,1)} %broadcast_in_dim.20), calls=%async_computation | async-start | bytes 393216 | tf_op jit(solution)/shard_map/all_to_all | solution.py:42
  9.8 0.7 copy.11.position
  10.5 0.0 copy-start.2
  10.5 0.9 copy-done.2
  11.4 0.1 shard_map.105
  11.6 3.1 %collective-permute-start = (bf16[64,1280]{1,0:T(8,128)(2,1)S(1)}, bf16[64,1280]{1,0:T(8,128)(2,1)S(1)}, u32[]{:S(2)}, u32[]{:S(2)}) collective-permute-start(bf16[64,1280]{1,0:T(8,128)(2,1)S(1)} %shard_map.105), channel_id=1, source_target_pairs={{0,8},{8,16},{16,24},{24,0},{1,9},{9,17},{17,25},{25,1},{2,10},{10... | collective-permute-start | bytes 491528 | tf_op jit(solution)/shard_map/ppermute | solution.py:51
  14.7 4.4 %collective-permute-start.1 = (bf16[64,1280]{1,0:T(8,128)(2,1)S(1)}, bf16[64,1280]{1,0:T(8,128)(2,1)S(1)}, u32[]{:S(2)}, u32[]{:S(2)}) collective-permute-start(bf16[64,1280]{1,0:T(8,128)(2,1)S(1)} %shard_map.105), channel_id=1, source_target_pairs={{0,16},{8,24},{16,0},{24,8},{1,17},{9,25},{17,1},{25,9},{2,18},{10... | collective-permute-start | bytes 491528 | tf_op jit(solution)/shard_map/ppermute | solution.py:51
  19.1 3.1 %collective-permute-start.2 = (bf16[64,1280]{1,0:T(8,128)(2,1)S(1)}, bf16[64,1280]{1,0:T(8,128)(2,1)S(1)}, u32[]{:S(2)}, u32[]{:S(2)}) collective-permute-start(bf16[64,1280]{1,0:T(8,128)(2,1)S(1)} %shard_map.105), channel_id=1, source_target_pairs={{0,24},{8,0},{16,8},{24,16},{1,25},{9,1},{17,9},{25,17},{2,26},{10... | collective-permute-start | bytes 491528 | tf_op jit(solution)/shard_map/ppermute | solution.py:51
  22.1 0.7 broadcast_in_dim.22.b2
  22.8 0.7 broadcast_in_dim.21.b1
  23.5 0.0 all-to-all-done.gathered
  23.5 0.0 copy-start
  23.5 1.5 %copy-done = bf16[1152,768]{1,0:T(8,128)(2,1)S(1)} copy-done((bf16[1152,768]{1,0:T(8,128)(2,1)S(1)}, bf16[1152,768]{1,0:T(8,128)(2,1)}, u32[]{:S(2)}) %copy-start) | copy-done | bytes 1769496
  25.0 0.0 copy-start.1
  25.0 1.5 %copy-done.1 = bf16[768,1152]{1,0:T(8,128)(2,1)S(1)} copy-done((bf16[768,1152]{1,0:T(8,128)(2,1)S(1)}, bf16[768,1152]{1,0:T(8,128)(2,1)}, u32[]{:S(2)}) %copy-start.1) | copy-done | bytes 1769496
  26.5 1.1 shard_map.104
  27.6 0.0 collective-permute-done
  27.6 0.0 collective-permute-done.1
  27.6 0.0 collective-permute-done.2
  27.7 3.7 %collective-permute-start.3 = (bf16[256,1280]{1,0:T(8,128)(2,1)S(1)}, bf16[256,1280]{1,0:T(8,128)(2,1)S(1)}, u32[]{:S(2)}, u32[]{:S(2)}) collective-permute-start(bf16[256,1280]{1,0:T(8,128)(2,1)S(1)} %constant_dynamic-update-slice_fusion.image_own), channel_id=1, source_target_pairs={{0,4},{4,0},{1,5},{5,1},{2,6},{6,2},{3,7},{7,3},{8,12},{12,8},{9,1... | collective-permute-start | bytes 1966088 | tf_op jit(solution)/shard_map/ppermute | solution.py:46
  31.4 17.4 %all_to_all.20.parts = f32[4,16,1152]{2,1,0:T(8,128)S(1)} all-to-all(f32[4,16,1152]{2,1,0:T(8,128)S(1)} %shard_map.104), channel_id=1, replica_groups=mesh['yl'=2,'z'=8,'x'=4,'core'=2,'t'=4] {'t'}, dimensions={0} | all-to-all | bytes 589824 | tf_op jit(solution)/shard_map/all_to_all | solution.py:189
  48.8 0.0 collective-permute-done.3.image_other
  48.8 0.1 shard_map.106
  49.0 26.8 %all_to_all.21.text_own = bf16[16,16,1152]{2,1,0:T(8,128)(2,1)S(1)} all-to-all(bf16[16,16,1152]{2,1,0:T(8,128)(2,1)S(1)} %shard_map.106), channel_id=1, replica_groups=mesh['yl'=2,'z'=8,'x'=4,'core'=2,'t'=4] {'yl','z'}, dimensions={0} | all-to-all | bytes 1179648 | tf_op jit(solution)/shard_map/all_to_all | solution.py:194
  75.8 4.7 %collective-permute-start.4 = (bf16[16,16,1152]{2,1,0:T(8,128)(2,1)S(1)}, bf16[16,16,1152]{2,1,0:T(8,128)(2,1)S(1)}, u32[]{:S(2)}, u32[]{:S(2)}) collective-permute-start(bf16[16,16,1152]{2,1,0:T(8,128)(2,1)S(1)} %all_to_all.21.text_own), channel_id=1, source_target_pairs={{0,4},{4,0},{1,5},{5,1},{2,6},{6,2},{3,7},{7,3},{8,12},{12,8},{9,1... | collective-permute-start | bytes 1769480 | tf_op jit(solution)/shard_map/ppermute | solution.py:46
  81.7 0.1 pad_add_fusion.place
  81.8 0.1 pad_maximum_fusion.numbers
  81.9 0.2 collective-permute-done.4.text_other
  82.0 2.5 %shard_map.107 = bf16[16,2,16,1152]{3,2,1,0:T(8,128)(2,1)S(1)} custom-call(s32[3]{0:T(128)S(1)} %pad_add_fusion.place, f32[2]{0:T(128)S(1)} %pad_maximum_fusion.numbers, bf16[16,16,1152]{2,1,0:T(8,128)(2,1)S(1)} %all_to_all.21.text_own, bf16[16,16,1152]{2,1,0:T(8,128)(2,1)S(1)} %collective-permute-done.4.text_other, ...), custom_call_target="tpu_custom_call" | custom-call | flops 1200000000 | bytes 100000 | tf_op jit(solution)/shard_map/pallas_call | solution.py:30
  84.5 26.0 %all_to_all.22.parts = bf16[16,2,16,1152]{3,2,1,0:T(8,128)(2,1)S(1)} all-to-all(bf16[16,2,16,1152]{3,2,1,0:T(8,128)(2,1)S(1)} %shard_map.107), channel_id=1, replica_groups={{0,32,64,96,128,160,192,224,256,288,320,352,384,416,448,480},{1,33,65,9..., dimensions={0} | all-to-all | bytes 2359296 | tf_op jit(solution)/shard_map/all_to_all | solution.py:204
  110.5 0.2 shard_map.108
  110.6 2.6 %collective-permute-start.5 = (f32[16,1152]{1,0:T(8,128)S(1)}, f32[16,1152]{1,0:T(8,128)S(1)}, u32[]{:S(2)}, u32[]{:S(2)}) collective-permute-start(f32[16,1152]{1,0:T(8,128)S(1)} %get-tuple-element.19), channel_id=1, source_target_pairs={{0,4},{4,0},{1,5},{5,1},{2,6},{6,2},{3,7},{7,3},{8,12},{12,8},{9,1... | collective-permute-start | bytes 221192 | tf_op jit(solution)/shard_map/ppermute | solution.py:46
  113.3 0.9 collective-permute-done.5
  114.2 0.7 broadcast_select_fusion
  (4 shorter events, 0.1 us)
Async XLA Ops:
  2.1 21.4 %all-to-all-start = ((bf16[4,64,288]{2,1,0:T(8,128)(2,1)}), bf16[4,64,288]{2,1,0:T(8,128)(2,1)S(1)}, u32[]{:S(2)}, u32[]{:S(2)}) async-start(bf16[4,64,288]{2,1,0:T(8,128)(2,1)} %broadcast_in_dim.20), calls=%async_computation | async-start | bytes 393216 | tf_op jit(solution)/shard_map/all_to_all | solution.py:42
  10.5 0.9 copy-start.2
  11.6 16.0 %collective-permute-start = (bf16[64,1280]{1,0:T(8,128)(2,1)S(1)}, bf16[64,1280]{1,0:T(8,128)(2,1)S(1)}, u32[]{:S(2)}, u32[]{:S(2)}) collective-permute-start(bf16[64,1280]{1,0:T(8,128)(2,1)S(1)} %shard_map.105), channel_id=1, source_target_pairs={{0,8},{8,16},{16,24},{24,0},{1,9},{9,17},{17,25},{25,1},{2,10},{10... | collective-permute-start | bytes 491528 | tf_op jit(solution)/shard_map/ppermute | solution.py:51
  14.7 12.9 %collective-permute-start.1 = (bf16[64,1280]{1,0:T(8,128)(2,1)S(1)}, bf16[64,1280]{1,0:T(8,128)(2,1)S(1)}, u32[]{:S(2)}, u32[]{:S(2)}) collective-permute-start(bf16[64,1280]{1,0:T(8,128)(2,1)S(1)} %shard_map.105), channel_id=1, source_target_pairs={{0,16},{8,24},{16,0},{24,8},{1,17},{9,25},{17,1},{25,9},{2,18},{10... | collective-permute-start | bytes 491528 | tf_op jit(solution)/shard_map/ppermute | solution.py:51
  19.1 8.5 %collective-permute-start.2 = (bf16[64,1280]{1,0:T(8,128)(2,1)S(1)}, bf16[64,1280]{1,0:T(8,128)(2,1)S(1)}, u32[]{:S(2)}, u32[]{:S(2)}) collective-permute-start(bf16[64,1280]{1,0:T(8,128)(2,1)S(1)} %shard_map.105), channel_id=1, source_target_pairs={{0,24},{8,0},{16,8},{24,16},{1,25},{9,1},{17,9},{25,17},{2,26},{10... | collective-permute-start | bytes 491528 | tf_op jit(solution)/shard_map/ppermute | solution.py:51
  23.5 1.5 %copy-start = (bf16[1152,768]{1,0:T(8,128)(2,1)S(1)}, bf16[1152,768]{1,0:T(8,128)(2,1)}, u32[]{:S(2)}) copy-start(bf16[1152,768]{1,0:T(8,128)(2,1)} %w1.1) | copy-start | bytes 5308420
  25.0 1.5 %copy-start.1 = (bf16[768,1152]{1,0:T(8,128)(2,1)S(1)}, bf16[768,1152]{1,0:T(8,128)(2,1)}, u32[]{:S(2)}) copy-start(bf16[768,1152]{1,0:T(8,128)(2,1)} %w2.1) | copy-start | bytes 5308420
  27.7 21.1 %collective-permute-start.3 = (bf16[256,1280]{1,0:T(8,128)(2,1)S(1)}, bf16[256,1280]{1,0:T(8,128)(2,1)S(1)}, u32[]{:S(2)}, u32[]{:S(2)}) collective-permute-start(bf16[256,1280]{1,0:T(8,128)(2,1)S(1)} %constant_dynamic-update-slice_fusion.image_own), channel_id=1, source_target_pairs={{0,4},{4,0},{1,5},{5,1},{2,6},{6,2},{3,7},{7,3},{8,12},{12,8},{9,1... | collective-permute-start | bytes 1966088 | tf_op jit(solution)/shard_map/ppermute | solution.py:46
  75.8 6.3 %collective-permute-start.4 = (bf16[16,16,1152]{2,1,0:T(8,128)(2,1)S(1)}, bf16[16,16,1152]{2,1,0:T(8,128)(2,1)S(1)}, u32[]{:S(2)}, u32[]{:S(2)}) collective-permute-start(bf16[16,16,1152]{2,1,0:T(8,128)(2,1)S(1)} %all_to_all.21.text_own), channel_id=1, source_target_pairs={{0,4},{4,0},{1,5},{5,1},{2,6},{6,2},{3,7},{7,3},{8,12},{12,8},{9,1... | collective-permute-start | bytes 1769480 | tf_op jit(solution)/shard_map/ppermute | solution.py:46
  110.6 3.5 %collective-permute-start.5 = (f32[16,1152]{1,0:T(8,128)S(1)}, f32[16,1152]{1,0:T(8,128)S(1)}, u32[]{:S(2)}, u32[]{:S(2)}) collective-permute-start(f32[16,1152]{1,0:T(8,128)S(1)} %get-tuple-element.19), channel_id=1, source_target_pairs={{0,4},{4,0},{1,5},{5,1},{2,6},{6,2},{3,7},{7,3},{8,12},{12,8},{9,1... | collective-permute-start | bytes 221192 | tf_op jit(solution)/shard_map/ppermute | solution.py:46

commit v3 on v2

--- a/solution.py
+++ b/solution.py
@@ -15,6 +15,8 @@
 F32 = jnp.float32
 LANES = 128
 VMEM = pl.BlockSpec(memory_space=pltpu.VMEM)
+HBM = pl.BlockSpec(memory_space=pl.ANY)
+FULL = 55_000_000
 SMEM = pl.BlockSpec(memory_space=pltpu.SMEM)
 
 
@@ -26,20 +28,16 @@
     return jnp.dot(a, b, preferred_element_type=F32)
 
 
-def call(kernel, outs, operands, scalars=0, flops=0):
+def call(kernel, outs, operands, scalars=0, flops=0, specs=None, out_specs=None, scratch=(), room=2**25):
     return pl.pallas_call(
         kernel,
         out_shape=outs,
-        in_specs=[SMEM] * scalars + [VMEM] * (len(operands) - scalars),
-        out_specs=jax.tree.map(lambda _: VMEM, outs),
-        compiler_params=pltpu.CompilerParams(vmem_limit_bytes=40 * 2**20),
+        in_specs=specs or [SMEM] * scalars + [VMEM] * (len(operands) - scalars),
+        out_specs=out_specs or jax.tree.map(lambda _: VMEM, outs),
+        scratch_shapes=scratch,
+        compiler_params=pltpu.CompilerParams(vmem_limit_bytes=room),
         cost_estimate=pl.CostEstimate(flops=flops, bytes_accessed=100_000, transcendentals=0),
     )(*operands)
-
-
-def spread(block, axes):
-    count = lax.axis_size(axes)
-    return lax.all_to_all(jnp.broadcast_to(block[None], (count,) + block.shape), axes, 0, 0)
 
 
 def swap_cores(block):
@@ -67,31 +65,40 @@
     return (values * lax.rsqrt(squared + EPSILON)).astype(BF16)
 
 
-def pack_kernel(pictures, position, packed):
-    width = pictures.shape[1]
+def pack_kernel(pictures, small, packed):
+    count, width = pictures.shape
     packed[:, :width] = unit(pictures[...].astype(F32))
-    where = position[...]
-    lane = lax.broadcasted_iota(jnp.int32, (where.shape[0], LANES), 1)
+    down = lax.broadcasted_iota(jnp.int32, (count, LANES), 0)
+    lane = lax.broadcasted_iota(jnp.int32, (count, LANES), 1)
+    where = jnp.sum(jnp.where(down == lane, small[:, :LANES], 0.0), axis=1, keepdims=True).astype(jnp.int32)
     digits = jnp.where(lane == 0, where // LANES, jnp.where(lane == 1, where % LANES, 0))
     packed[:, width:] = digits.astype(F32).astype(BF16)
 
 
-def ffn_kernel(first, gathered, w1, b1, w2, b2, partial):
-    parts = [gathered[k].astype(F32) for k in range(gathered.shape[0])]
-    tokens = jnp.concatenate(parts, axis=1)
+def ffn_kernel(gathered, small, w1, w2, partial, w1_near, w2_near, sems):
+    first = pltpu.make_async_copy(w1, w1_near, sems.at[0])
+    second = pltpu.make_async_copy(w2, w2_near, sems.at[1])
+    first.start()
+    second.start()
+    hid = w1.shape[1]
+    b1, b2 = small[:, LANES : LANES + hid], small[:, LANES + hid :]
+    count = gathered.shape[0]
+    tokens = jnp.concatenate([gathered[k].astype(F32) for k in range(count)], axis=1)
     centred = tokens - jnp.mean(tokens, axis=-1, keepdims=True)
     variance = jnp.mean(centred * centred, axis=-1, keepdims=True)
     normed = (centred * lax.rsqrt(variance + EPSILON)).astype(BF16)
-    hidden = jax.nn.gelu(nn(normed, w1[...]) + b1[...], approximate=True).astype(BF16)
-    branch = nn(hidden, w2[...])
-    kept = jnp.where(first[0] == 0, tokens + b2[...], 0.0)
-    partial[...] = (branch + kept).reshape(partial.shape)
+    first.wait()
+    hidden = jax.nn.gelu(nn(normed, w1_near[...]) + b1, approximate=True).astype(BF16)
+    second.wait()
+    branch = nn(hidden, w2_near[...])
+    total = branch + (tokens + b2) * (1.0 / count)
+    partial[...] = total.reshape(partial.shape).astype(partial.dtype)
 
 
 def text_kernel(parts, copies):
-    total = parts[0]
+    total = parts[0].astype(F32)
     for k in range(1, parts.shape[0]):
-        total = total + parts[k]
+        total = total + parts[k].astype(F32)
     row = unit(total)
     for k in range(copies.shape[0]):
         copies[k] = row
@@ -152,16 +159,17 @@
                 out[pl.ds(at * tensor, tensor), 1 - which] = rows
 
 
-def sum_kernel(core, parts, keep, send):
-    def total(which):
-        value = parts[0, which].astype(F32)
-        for k in range(1, parts.shape[0]):
-            value = value + parts[k, which].astype(F32)
-        return value
-
-    first, second = total(0), total(1)
-    keep[...] = jnp.where(core[0] == 0, first, second)
-    send[...] = jnp.where(core[0] == 0, second, first)
+def sum_kernel(parts, total):
+    value = parts[0].astype(F32)
+    for k in range(1, parts.shape[0]):
+        value = value + parts[k].astype(F32)
+    total[...] = value
+
+
+def pick_kernel(place, both, text, image):
+    core = place[1]
+    text[...] = both[0, pl.ds(core, 1)][0]
+    image[...] = both[1, pl.ds(core, 1)][0]
 
 
 def shards(tokens, w1, b1, w2, b2, pictures, matching, sharpness, offset):
@@ -172,28 +180,31 @@
     own = rows // tensor
     groups = lax.axis_size(("yl", "z"))
 
-    gathered = spread(tokens, "t")
-    packed = call(
-        pack_kernel,
-        jax.ShapeDtypeStruct((rows, width + LANES), BF16),
-        (pictures, matching[:, None]),
-    )
+    bf16, f32 = (functools.partial(jax.ShapeDtypeStruct, dtype=d) for d in (BF16, F32))
+    to_all = jnp.broadcast_to(tokens[None], (tensor,) + tokens.shape)
+    gathered = lax.all_to_all(to_all, "t", 0, 0)
+    spots = jnp.pad(matching.astype(F32), (0, LANES - rows))
+    small = jnp.concatenate([spots, b1, b2])[None]
+    packed = call(pack_kernel, bf16((rows, width + LANES)), (pictures, small))
     moved = [from_behind(packed, k) for k in range(1, ring)]
+    numbers = jnp.concatenate([sharpness, offset])
     partial = call(
         ffn_kernel,
-        jax.ShapeDtypeStruct((tensor, own, width), F32),
-        (t[None], gathered, w1, b1[None], w2, b2[None]),
-        scalars=1,
+        bf16((tensor, own, width)),
+        (gathered, small, w1, w2),
+        specs=[VMEM, VMEM, HBM, HBM],
+        scratch=[pltpu.VMEM(a.shape, a.dtype) for a in (w1, w2)]
+        + [pltpu.SemaphoreType.DMA((2,))],
+        room=FULL,
     )
     partial, packed, *moved = lax.optimization_barrier((partial, packed, *moved))
     parts = lax.all_to_all(partial, "t", 0, 0)
     image_own = jnp.concatenate([packed] + moved, axis=0)
     image_other = swap_cores(image_own)
     parts, image_other = lax.optimization_barrier((parts, image_other))
-    copies = call(text_kernel, jax.ShapeDtypeStruct((groups, own, width), BF16), (parts,))
+    copies = call(text_kernel, bf16((groups, own, width)), (parts,))
     text_own = lax.all_to_all(copies, ("yl", "z"), 0, 0)
     text_other = swap_cores(text_own)
-    numbers = jnp.concatenate([sharpness, offset])
     shares = call(
         pair_kernel,
         jax.ShapeDtypeStruct((groups, 2, own, width), BF16),
@@ -202,10 +213,10 @@
         flops=1_200_000_000,
     )
     shares = lax.all_to_all(shares, ALL, 0, 0, axis_index_groups=grad_groups())
-    half = jax.ShapeDtypeStruct((own, width), F32)
-    keep, send = call(sum_kernel, (half, half), (core[None], shares), scalars=1)
-    came = swap_cores(send)
-    return jnp.where(core == 0, keep, came), jnp.where(core == 0, came, keep)
+    total = call(sum_kernel, f32((2, own, width)), (shares,))
+    both = lax.all_gather(total, "core")
+    half = f32((own, width))
+    return tuple(call(pick_kernel, (half, half), (place, both), scalars=1))
 
 
 def solution(mesh):

time: 116 us -> 112 us (0.966)
  local copies, waits for them, and re-layouts: 7.54 us -> 2.45 us
  starting transfers between devices: 29.2 us -> 25 us
  waiting for transfers between devices: 1.05 us -> 4.82 us
  Pallas kernels: 4.01 us -> 6.67 us
  blocking collectives: 70.2 us -> 69 us
    ppermute x3, waiting for transfers between devices: 0.01 us -> 4.65 us  [from_behind(): lax.ppermute(block, 'x', [(i, (i + by) % length) for i in range(length)])]
    all_to_all x1, blocking collectives: 17.4 us -> 14.4 us  [shards(): parts = lax.all_to_all(partial, 't', 0, 0)]
    ppermute x3 -> x2, starting transfers between devices: 11 us -> 7.99 us  [swap_cores(): return lax.ppermute(block, 'core', [(0, 1), (1, 0)])]
    unnamed x9 -> x5, local copies, waits for them, and re-layouts: 3.9 us -> 0.95 us
    all_gather x0 -> x1, blocking collectives: none -> 2.81 us  [shards(): both = lax.all_gather(total, 'core')]
    pallas_call x5 -> x6, Pallas kernels: 4.01 us -> 6.67 us  [call(): pl.pallas_call(kernel, out_shape=outs, in_specs=specs or [SMEM] * scalars...]
    broadcast_in_dim x4 -> x1, local copies, waits for them, and re-layouts: 3.63 us -> 1.49 us  [shards(): to_all = jnp.broadcast_to(tokens[None], (tensor,) + tokens.shape)]
    ppermute x3, starting transfers between devices: 10.5 us -> 9.33 us  [from_behind(): lax.ppermute(block, 'x', [(i, (i + by) % length) for i in range(length)])]
  transfers between devices with their start and end apart: 7 -> 6, of which waited for: 2 -> 2; matrix products, arithmetic and copies ran while one was open for 2% -> 1% of each run, Pallas kernels for 1% -> 2%
where the time goes in v3:
time: 112 us; the launch traced here: 111 us
  blocking collectives  69 us (62%)
  starting transfers between devices  25 us (22%)
  Pallas kernels  6.67 us (6%)
  waiting for transfers between devices  4.82 us (4%)
  local copies, waits for them, and re-layouts  2.45 us (2%)
  between operations  2.05 us (2%)
  other arithmetic  1.52 us (1%)
    all_to_all x1, blocking collectives, shards(): text_own = lax.all_to_all(copies, ('yl', 'z'), 0, 0)  27 us
    all_to_all x1, blocking collectives, shards(): shares = lax.all_to_all(shares, ALL, 0, 0, axis_index_groups=grad_groups())  24.9 us
    all_to_all x1, blocking collectives, shards(): parts = lax.all_to_all(partial, 't', 0, 0)  14.4 us
    ppermute x3, starting transfers between devices, from_behind(): lax.ppermute(block, 'x', [(i, (i + by) % length) for i in range(length)])  9.33 us
    ppermute x2, starting transfers between devices, swap_cores(): return lax.ppermute(block, 'core', [(0, 1), (1, 0)])  7.99 us
    all_to_all x1, starting transfers between devices, shards(): gathered = lax.all_to_all(to_all, 't', 0, 0)  7.64 us
    pallas_call x6, Pallas kernels, call(): pl.pallas_call(kernel, out_shape=outs, in_specs=specs or [SMEM] * scalars...  6.67 us
    ppermute x3, waiting for transfers between devices, from_behind(): lax.ppermute(block, 'x', [(i, (i + by) % length) for i in range(length)])  4.65 us
  transfers between devices with their start and end apart: 6, of which 2 were waited for; matrix products, arithmetic and copies ran while one was open for 1% of the time, Pallas kernels for 2%

profile of v3, /device:TPU:1, one launch (start us, length us, event | category | flops | bytes accessed | tf_op | source)
XLA Modules:
  0.0 111.5 jit_solution(5749771710441510285)
XLA Ops:
  0.6 1.5 %broadcast_in_dim.4 = bf16[4,64,288]{2,1,0:T(8,128)(2,1)} broadcast(bf16[64,288]{1,0:T(8,128)(2,1)} %param.9), dimensions={1,2} | broadcast | bytes 184320 | tf_op jit(solution)/shard_map/broadcast_in_dim | solution.py:184
  2.1 7.6 %all-to-all-start = ((bf16[4,64,288]{2,1,0:T(8,128)(2,1)}), bf16[4,64,288]{2,1,0:T(8,128)(2,1)S(1)}, u32[]{:S(2)}, u32[]{:S(2)}) async-start(bf16[4,64,288]{2,1,0:T(8,128)(2,1)} %broadcast_in_dim.4), calls=%async_computation | async-start | bytes 393216 | tf_op jit(solution)/shard_map/all_to_all | solution.py:185
  9.8 0.7 convert_element_type.5
  10.4 0.7 fusion
  11.1 0.0 copy-start
  11.1 0.9 copy-done
  12.0 0.1 shard_map.105
  12.2 4.4 %collective-permute-start.2 = (bf16[64,1280]{1,0:T(8,128)(2,1)S(1)}, bf16[64,1280]{1,0:T(8,128)(2,1)S(1)}, u32[]{:S(2)}, u32[]{:S(2)}) collective-permute-start(bf16[64,1280]{1,0:T(8,128)(2,1)S(1)} %shard_map.105), channel_id=1, source_target_pairs={{0,24},{8,0},{16,8},{24,16},{1,25},{9,1},{17,9},{25,17},{2,26},{10... | collective-permute-start | bytes 491528 | tf_op jit(solution)/shard_map/ppermute | solution.py:49
  16.6 2.4 %collective-permute-start.1 = (bf16[64,1280]{1,0:T(8,128)(2,1)S(1)}, bf16[64,1280]{1,0:T(8,128)(2,1)S(1)}, u32[]{:S(2)}, u32[]{:S(2)}) collective-permute-start(bf16[64,1280]{1,0:T(8,128)(2,1)S(1)} %shard_map.105), channel_id=1, source_target_pairs={{0,16},{8,24},{16,0},{24,8},{1,17},{9,25},{17,1},{25,9},{2,18},{10... | collective-permute-start | bytes 491528 | tf_op jit(solution)/shard_map/ppermute | solution.py:49
  19.0 2.5 %collective-permute-start = (bf16[64,1280]{1,0:T(8,128)(2,1)S(1)}, bf16[64,1280]{1,0:T(8,128)(2,1)S(1)}, u32[]{:S(2)}, u32[]{:S(2)}) collective-permute-start(bf16[64,1280]{1,0:T(8,128)(2,1)S(1)} %shard_map.105), channel_id=1, source_target_pairs={{0,8},{8,16},{16,24},{24,0},{1,9},{9,17},{17,25},{25,1},{2,10},{10... | collective-permute-start | bytes 491528 | tf_op jit(solution)/shard_map/ppermute | solution.py:49
  21.5 0.0 all-to-all-done.gathered
  21.5 2.5 %shard_map.104 = bf16[4,16,1152]{2,1,0:T(8,128)(2,1)S(1)} custom-call(bf16[4,64,288]{2,1,0:T(8,128)(2,1)S(1)} %all-to-all-done.gathered, f32[1,2048]{1,0:T(1,128)S(1)} %bitcast.7, bf16[1152,768]{1,0:T(8,128)(2,1)} %w1.1, bf16[768,1152]{1,0:T(8,128)(2,1)} %w2.1), custom_call_target="tpu_custom_call" | custom-call | bytes 100000 | tf_op jit(solution)/shard_map/pallas_call | solution.py:32
  24.1 0.0 collective-permute-done.2
  24.1 0.0 collective-permute-done.1
  24.1 4.6 %collective-permute-done = bf16[64,1280]{1,0:T(8,128)(2,1)S(1)} collective-permute-done((bf16[64,1280]{1,0:T(8,128)(2,1)S(1)}, bf16[64,1280]{1,0:T(8,128)(2,1)S(1)}, u32[]{:S(2)}, u32[]{:S(2)}) %collective-permute-start) | collective-permute-done | bytes 163872 | tf_op jit(solution)/shard_map/ppermute | solution.py:49
  28.8 3.4 %collective-permute-start.3 = (bf16[256,1280]{1,0:T(8,128)(2,1)S(1)}, bf16[256,1280]{1,0:T(8,128)(2,1)S(1)}, u32[]{:S(2)}, u32[]{:S(2)}) collective-permute-start(bf16[256,1280]{1,0:T(8,128)(2,1)S(1)} %constant_dynamic-update-slice_fusion.image_own), channel_id=1, source_target_pairs={{0,4},{4,0},{1,5},{5,1},{2,6},{6,2},{3,7},{7,3},{8,12},{12,8},{9,1... | collective-permute-start | bytes 1966088 | tf_op jit(solution)/shard_map/ppermute | solution.py:44
  32.2 14.4 %all_to_all.20.parts = bf16[4,16,1152]{2,1,0:T(8,128)(2,1)S(1)} all-to-all(bf16[4,16,1152]{2,1,0:T(8,128)(2,1)S(1)} %shard_map.104), channel_id=1, replica_groups=mesh['yl'=2,'z'=8,'x'=4,'core'=2,'t'=4] {'t'}, dimensions={0} | all-to-all | bytes 294912 | tf_op jit(solution)/shard_map/all_to_all | solution.py:201
  46.6 0.0 collective-permute-done.3.image_other
  46.6 0.1 shard_map.106
  46.7 27.0 %all_to_all.21.text_own = bf16[16,16,1152]{2,1,0:T(8,128)(2,1)S(1)} all-to-all(bf16[16,16,1152]{2,1,0:T(8,128)(2,1)S(1)} %shard_map.106), channel_id=1, replica_groups=mesh['yl'=2,'z'=8,'x'=4,'core'=2,'t'=4] {'yl','z'}, dimensions={0} | all-to-all | bytes 1179648 | tf_op jit(solution)/shard_map/all_to_all | solution.py:206
  73.7 4.6 %collective-permute-start.4 = (bf16[16,16,1152]{2,1,0:T(8,128)(2,1)S(1)}, bf16[16,16,1152]{2,1,0:T(8,128)(2,1)S(1)}, u32[]{:S(2)}, u32[]{:S(2)}) collective-permute-start(bf16[16,16,1152]{2,1,0:T(8,128)(2,1)S(1)} %all_to_all.21.text_own), channel_id=1, source_target_pairs={{0,4},{4,0},{1,5},{5,1},{2,6},{6,2},{3,7},{7,3},{8,12},{12,8},{9,1... | collective-permute-start | bytes 1769480 | tf_op jit(solution)/shard_map/ppermute | solution.py:44
  79.6 0.1 pad_maximum_fusion.numbers
  79.7 0.1 pad_add_fusion.place
  79.8 0.2 collective-permute-done.4.text_other
  80.0 2.5 %shard_map.107 = bf16[16,2,16,1152]{3,2,1,0:T(8,128)(2,1)S(1)} custom-call(s32[3]{0:T(128)S(1)} %pad_add_fusion.place, f32[2]{0:T(128)S(1)} %pad_maximum_fusion.numbers, bf16[16,16,1152]{2,1,0:T(8,128)(2,1)S(1)} %all_to_all.21.text_own, bf16[16,16,1152]{2,1,0:T(8,128)(2,1)S(1)} %collective-permute-done.4.text_other, ...), custom_call_target="tpu_custom_call" | custom-call | flops 1200000000 | bytes 100000 | tf_op jit(solution)/shard_map/pallas_call | solution.py:32
  82.4 24.9 %all_to_all.22.parts = bf16[16,2,16,1152]{3,2,1,0:T(8,128)(2,1)S(1)} all-to-all(bf16[16,2,16,1152]{3,2,1,0:T(8,128)(2,1)S(1)} %shard_map.107), channel_id=1, replica_groups={{0,32,64,96,128,160,192,224,256,288,320,352,384,416,448,480},{1,33,65,9..., dimensions={0} | all-to-all | bytes 2359296 | tf_op jit(solution)/shard_map/all_to_all | solution.py:215
  107.3 0.2 shard_map.108
  107.5 2.8 %all-gather = f32[4,16,1152]{2,1,0:T(8,128)S(1)} all-gather(f32[2,16,1152]{2,1,0:T(8,128)S(1)} %shard_map.108), channel_id=2, replica_groups=mesh['yl'=2,'z'=8,'x'=4,'core'=2,'t'=4] {'core'}, dimensions={0}, use_global_device_ids=true | all-gather | bytes 442368 | tf_op jit(solution)/shard_map/all_gather | solution.py:217
  110.3 1.2 %shard_map.109 = (f32[16,1152]{1,0:T(8,128)}, f32[16,1152]{1,0:T(8,128)}) custom-call(s32[3]{0:T(128)S(1)} %pad_add_fusion.place, f32[2,2,16,1152]{3,2,1,0:T(8,128)S(1)} %bitcast.5), custom_call_target="tpu_custom_call" | custom-call | bytes 100000 | tf_op jit(solution)/shard_map/pallas_call | solution.py:32
  (4 shorter events, 0.1 us)
Async XLA Ops:
  2.1 19.4 %all-to-all-start = ((bf16[4,64,288]{2,1,0:T(8,128)(2,1)}), bf16[4,64,288]{2,1,0:T(8,128)(2,1)S(1)}, u32[]{:S(2)}, u32[]{:S(2)}) async-start(bf16[4,64,288]{2,1,0:T(8,128)(2,1)} %broadcast_in_dim.4), calls=%async_computation | async-start | bytes 393216 | tf_op jit(solution)/shard_map/all_to_all | solution.py:185
  11.1 0.9 copy-start
  12.2 11.9 %collective-permute-start.2 = (bf16[64,1280]{1,0:T(8,128)(2,1)S(1)}, bf16[64,1280]{1,0:T(8,128)(2,1)S(1)}, u32[]{:S(2)}, u32[]{:S(2)}) collective-permute-start(bf16[64,1280]{1,0:T(8,128)(2,1)S(1)} %shard_map.105), channel_id=1, source_target_pairs={{0,24},{8,0},{16,8},{24,16},{1,25},{9,1},{17,9},{25,17},{2,26},{10... | collective-permute-start | bytes 491528 | tf_op jit(solution)/shard_map/ppermute | solution.py:49
  16.6 7.6 %collective-permute-start.1 = (bf16[64,1280]{1,0:T(8,128)(2,1)S(1)}, bf16[64,1280]{1,0:T(8,128)(2,1)S(1)}, u32[]{:S(2)}, u32[]{:S(2)}) collective-permute-start(bf16[64,1280]{1,0:T(8,128)(2,1)S(1)} %shard_map.105), channel_id=1, source_target_pairs={{0,16},{8,24},{16,0},{24,8},{1,17},{9,25},{17,1},{25,9},{2,18},{10... | collective-permute-start | bytes 491528 | tf_op jit(solution)/shard_map/ppermute | solution.py:49
  19.0 9.7 %collective-permute-start = (bf16[64,1280]{1,0:T(8,128)(2,1)S(1)}, bf16[64,1280]{1,0:T(8,128)(2,1)S(1)}, u32[]{:S(2)}, u32[]{:S(2)}) collective-permute-start(bf16[64,1280]{1,0:T(8,128)(2,1)S(1)} %shard_map.105), channel_id=1, source_target_pairs={{0,8},{8,16},{16,24},{24,0},{1,9},{9,17},{17,25},{25,1},{2,10},{10... | collective-permute-start | bytes 491528 | tf_op jit(solution)/shard_map/ppermute | solution.py:49
  28.8 17.8 %collective-permute-start.3 = (bf16[256,1280]{1,0:T(8,128)(2,1)S(1)}, bf16[256,1280]{1,0:T(8,128)(2,1)S(1)}, u32[]{:S(2)}, u32[]{:S(2)}) collective-permute-start(bf16[256,1280]{1,0:T(8,128)(2,1)S(1)} %constant_dynamic-update-slice_fusion.image_own), channel_id=1, source_target_pairs={{0,4},{4,0},{1,5},{5,1},{2,6},{6,2},{3,7},{7,3},{8,12},{12,8},{9,1... | collective-permute-start | bytes 1966088 | tf_op jit(solution)/shard_map/ppermute | solution.py:44
  73.7 6.2 %collective-permute-start.4 = (bf16[16,16,1152]{2,1,0:T(8,128)(2,1)S(1)}, bf16[16,16,1152]{2,1,0:T(8,128)(2,1)S(1)}, u32[]{:S(2)}, u32[]{:S(2)}) collective-permute-start(bf16[16,16,1152]{2,1,0:T(8,128)(2,1)S(1)} %all_to_all.21.text_own), channel_id=1, source_target_pairs={{0,4},{4,0},{1,5},{5,1},{2,6},{6,2},{3,7},{7,3},{8,12},{12,8},{9,1... | collective-permute-start | bytes 1769480 | tf_op jit(solution)/shard_map/ppermute | solution.py:44

commit v4 on v3

--- a/solution.py
+++ b/solution.py
@@ -44,9 +44,8 @@
     return lax.ppermute(block, "core", [(0, 1), (1, 0)])
 
 
-def from_behind(block, by):
-    length = lax.axis_size("x")
-    return lax.ppermute(block, "x", [(i, (i + by) % length) for i in range(length)])
+def swap_along_x(block, bit):
+    return lax.ppermute(block, "x", [(i, i ^ bit) for i in range(lax.axis_size("x"))])
 
 
 def grad_groups():
@@ -153,8 +152,8 @@
                 part = nn(weights(a, b, match), b)
                 total = part if total is None else total + part
             total = total.astype(BF16)
-            for k in range(ring):
-                at = lax.rem(x + ring - k, ring)
+            for k, bits in enumerate((0, 2, 1, 3)):
+                at = jnp.bitwise_xor(x, bits)
                 rows = total[k * block : (k + 1) * block].reshape(tensor, own, width)
                 out[pl.ds(at * tensor, tensor), 1 - which] = rows
 
@@ -166,17 +165,11 @@
     total[...] = value
 
 
-def pick_kernel(place, both, text, image):
-    core = place[1]
-    text[...] = both[0, pl.ds(core, 1)][0]
-    image[...] = both[1, pl.ds(core, 1)][0]
-
-
 def shards(tokens, w1, b1, w2, b2, pictures, matching, sharpness, offset):
     x, core, t = (lax.axis_index(a).astype(jnp.int32) for a in ("x", "core", "t"))
     place = jnp.stack([x, core, t])
     rows, width = pictures.shape
-    tensor, ring = lax.axis_size("t"), lax.axis_size("x")
+    tensor = lax.axis_size("t")
     own = rows // tensor
     groups = lax.axis_size(("yl", "z"))
 
@@ -186,7 +179,7 @@
     spots = jnp.pad(matching.astype(F32), (0, LANES - rows))
     small = jnp.concatenate([spots, b1, b2])[None]
     packed = call(pack_kernel, bf16((rows, width + LANES)), (pictures, small))
-    moved = [from_behind(packed, k) for k in range(1, ring)]
+    moved = swap_along_x(packed, 2)
     numbers = jnp.concatenate([sharpness, offset])
     partial = call(
         ffn_kernel,
@@ -197,13 +190,20 @@
         + [pltpu.SemaphoreType.DMA((2,))],
         room=FULL,
     )
-    partial, packed, *moved = lax.optimization_barrier((partial, packed, *moved))
+    partial, packed, moved = lax.optimization_barrier((partial, packed, moved))
+    couple = jnp.concatenate([packed, moved], axis=0)
+    partial, couple = lax.optimization_barrier((partial, couple))
+    moved = swap_along_x(couple, 1)
     parts = lax.all_to_all(partial, "t", 0, 0)
-    image_own = jnp.concatenate([packed] + moved, axis=0)
+    parts, couple, moved = lax.optimization_barrier((parts, couple, moved))
+    image_own = jnp.concatenate([couple, moved], axis=0)
+    copies = call(text_kernel, bf16((groups, own, width)), (parts,))
+    copies, image_own = lax.optimization_barrier((copies, image_own))
     image_other = swap_cores(image_own)
-    parts, image_other = lax.optimization_barrier((parts, image_other))
-    copies = call(text_kernel, bf16((groups, own, width)), (parts,))
     text_own = lax.all_to_all(copies, ("yl", "z"), 0, 0)
+    text_own, image_other, place, numbers, core = lax.optimization_barrier(
+        (text_own, image_other, place, numbers, core)
+    )
     text_other = swap_cores(text_own)
     shares = call(
         pair_kernel,
@@ -215,8 +215,10 @@
     shares = lax.all_to_all(shares, ALL, 0, 0, axis_index_groups=grad_groups())
     total = call(sum_kernel, f32((2, own, width)), (shares,))
     both = lax.all_gather(total, "core")
-    half = f32((own, width))
-    return tuple(call(pick_kernel, (half, half), (place, both), scalars=1))
+    own_row = functools.partial(
+        lax.dynamic_index_in_dim, index=core, keepdims=False, allow_negative_indices=False
+    )
+    return own_row(both[0]), own_row(both[1])
 
 
 def solution(mesh):

time: 112 us -> 103 us (0.920)
  blocking collectives: 69 us -> 42.1 us
  starting transfers between devices: 25 us -> 38.9 us
  waiting for transfers between devices: 4.82 us -> 8.63 us
    all_to_all x1 -> x0, blocking collectives: 27 us -> none  [shards(): text_own = lax.all_to_all(copies, ('yl', 'z'), 0, 0)]
    all_to_all x0 -> x1, starting transfers between devices: none -> 10.8 us  [shards(): text_own = lax.all_to_all(copies, ('yl', 'z'), 0, 0)]
    all_to_all x0 -> x1, waiting for transfers between devices: none -> 5.75 us  [shards(): text_own = lax.all_to_all(copies, ('yl', 'z'), 0, 0)]
    ppermute x2, starting transfers between devices: 7.99 us -> 12.7 us  [swap_cores(): return lax.ppermute(block, 'core', [(0, 1), (1, 0)])]
    ppermute x3 -> x2, waiting for transfers between devices: 4.65 us -> 0.01 us  [swap_along_x(): lax.ppermute(block, 'x', [(i, i ^ bit) for i in range(lax.axis_size('x'))])]
    all_to_all x1, blocking collectives: 24.9 us -> 26.7 us  [shards(): shares = lax.all_to_all(shares, ALL, 0, 0, axis_index_groups=grad_groups())]
    ppermute x2, waiting for transfers between devices: 0.16 us -> 1.86 us  [swap_cores(): return lax.ppermute(block, 'core', [(0, 1), (1, 0)])]
    ppermute x3 -> x2, starting transfers between devices: 9.33 us -> 7.69 us  [swap_along_x(): lax.ppermute(block, 'x', [(i, i ^ bit) for i in range(lax.axis_size('x'))])]
  transfers between devices with their start and end apart: 6 -> 6, of which waited for: 2 -> 4; matrix products, arithmetic and copies ran while one was open for 1% -> 1% of each run, Pallas kernels for 2% -> 3%
where the time goes in v4:
time: 103 us
  blocking collectives  42.1 us (41%)
  starting transfers between devices  38.9 us (38%)
  waiting for transfers between devices  8.63 us (8%)
  Pallas kernels  6.3 us (6%)
  local copies, waits for them, and re-layouts  3.09 us (3%)
  between operations  2.02 us (2%)
  other arithmetic  1.59 us (2%)
    all_to_all x1, blocking collectives, shards(): shares = lax.all_to_all(shares, ALL, 0, 0, axis_index_groups=grad_groups())  26.7 us
    all_to_all x1, blocking collectives, shards(): parts = lax.all_to_all(partial, 't', 0, 0)  13.2 us
    ppermute x2, starting transfers between devices, swap_cores(): return lax.ppermute(block, 'core', [(0, 1), (1, 0)])  12.7 us
    all_to_all x1, starting transfers between devices, shards(): text_own = lax.all_to_all(copies, ('yl', 'z'), 0, 0)  10.8 us
    ppermute x2, starting transfers between devices, swap_along_x(): lax.ppermute(block, 'x', [(i, i ^ bit) for i in range(lax.axis_size('x'))])  7.69 us
    all_to_all x1, starting transfers between devices, shards(): gathered = lax.all_to_all(to_all, 't', 0, 0)  7.64 us
    pallas_call x5, Pallas kernels, call(): pl.pallas_call(kernel, out_shape=outs, in_specs=specs or [SMEM] * scalars...  6.3 us
    all_to_all x1, waiting for transfers between devices, shards(): text_own = lax.all_to_all(copies, ('yl', 'z'), 0, 0)  5.75 us
  transfers between devices with their start and end apart: 6, of which 4 were waited for; matrix products, arithmetic and copies ran while one was open for 1% of the time, Pallas kernels for 3%

profile of v4, /device:TPU:1, one launch (start us, length us, event | category | flops | bytes accessed | tf_op | source)
XLA Modules:
  0.0 102.6 jit_solution(7492634226777791152)
XLA Ops:
  0.6 1.5 %broadcast_in_dim.4 = bf16[4,64,288]{2,1,0:T(8,128)(2,1)} broadcast(bf16[64,288]{1,0:T(8,128)(2,1)} %param.9), dimensions={1,2} | broadcast | bytes 184320 | tf_op jit(solution)/shard_map/broadcast_in_dim | solution.py:177
  2.1 7.6 %all-to-all-start = ((bf16[4,64,288]{2,1,0:T(8,128)(2,1)}), bf16[4,64,288]{2,1,0:T(8,128)(2,1)S(1)}, u32[]{:S(2)}, u32[]{:S(2)}) async-start(bf16[4,64,288]{2,1,0:T(8,128)(2,1)} %broadcast_in_dim.4), calls=%async_computation | async-start | bytes 393216 | tf_op jit(solution)/shard_map/all_to_all | solution.py:178
  9.8 0.7 convert_element_type.5
  10.4 0.7 fusion
  11.1 0.0 copy-start
  11.1 0.9 copy-done
  12.0 0.1 shard_map.105
  12.2 4.7 %collective-permute-start = (bf16[64,1280]{1,0:T(8,128)(2,1)S(1)}, bf16[64,1280]{1,0:T(8,128)(2,1)S(1)}, u32[]{:S(2)}, u32[]{:S(2)}) collective-permute-start(bf16[64,1280]{1,0:T(8,128)(2,1)S(1)} %shard_map.105), channel_id=1, source_target_pairs={{0,16},{8,24},{16,0},{24,8},{1,17},{9,25},{17,1},{25,9},{2,18},{10... | collective-permute-start | bytes 491528 | tf_op jit(solution)/shard_map/ppermute | solution.py:48
  16.8 1.0 all-to-all-done.gathered
  17.9 2.5 %shard_map.104 = bf16[4,16,1152]{2,1,0:T(8,128)(2,1)S(1)} custom-call(bf16[4,64,288]{2,1,0:T(8,128)(2,1)S(1)} %all-to-all-done.gathered, f32[1,2048]{1,0:T(1,128)S(1)} %bitcast.9, bf16[1152,768]{1,0:T(8,128)(2,1)} %w1.1, bf16[768,1152]{1,0:T(8,128)(2,1)} %w2.1), custom_call_target="tpu_custom_call" | custom-call | bytes 100000 | tf_op jit(solution)/shard_map/pallas_call | solution.py:32
  20.4 0.0 collective-permute-done
  20.4 3.0 %collective-permute-start.1 = (bf16[128,1280]{1,0:T(8,128)(2,1)S(1)}, bf16[128,1280]{1,0:T(8,128)(2,1)S(1)}, u32[]{:S(2)}, u32[]{:S(2)}) collective-permute-start(bf16[128,1280]{1,0:T(8,128)(2,1)S(1)} %pad_maximum_fusion.1), channel_id=1, source_target_pairs={{0,8},{8,0},{16,24},{24,16},{1,9},{9,1},{17,25},{25,17},{2,10},{10... | collective-permute-start | bytes 983048 | tf_op jit(solution)/shard_map/ppermute | solution.py:48
  23.5 13.2 %all_to_all.20.parts = bf16[4,16,1152]{2,1,0:T(8,128)(2,1)S(1)} all-to-all(bf16[4,16,1152]{2,1,0:T(8,128)(2,1)S(1)} %shard_map.104), channel_id=1, replica_groups=mesh['yl'=2,'z'=8,'x'=4,'core'=2,'t'=4] {'t'}, dimensions={0} | all-to-all | bytes 294912 | tf_op jit(solution)/shard_map/all_to_all | solution.py:197
  36.7 0.0 collective-permute-done.1
  36.7 1.0 shard_map.106
  37.7 10.8 %all-to-all-start.2 = ((bf16[16,16,1152]{2,1,0:T(8,128)(2,1)}), bf16[16,16,1152]{2,1,0:T(8,128)(2,1)S(1)}, u32[]{:S(2)}, u32[]{:S(2)}) async-start(bf16[16,16,1152]{2,1,0:T(8,128)(2,1)} %shard_map.106), calls=%async_computation.2 | async-start | bytes 1179648 | tf_op jit(solution)/shard_map/all_to_all | solution.py:203
  48.5 6.5 %collective-permute-start.2 = (bf16[256,1280]{1,0:T(8,128)(2,1)S(1)}, bf16[256,1280]{1,0:T(8,128)(2,1)S(1)}, u32[]{:S(2)}, u32[]{:S(2)}) collective-permute-start(bf16[256,1280]{1,0:T(8,128)(2,1)S(1)} %pad_maximum_fusion.image_own), channel_id=1, source_target_pairs={{0,4},{4,0},{1,5},{5,1},{2,6},{6,2},{3,7},{7,3},{8,12},{12,8},{9,1... | collective-permute-start | bytes 1966088 | tf_op jit(solution)/shard_map/ppermute | solution.py:44
  56.3 0.1 pad_maximum_fusion.2.numbers
  56.4 0.1 pad_add_fusion.place
  56.4 0.3 collective-permute-done.2.image_other
  56.7 5.7 %all-to-all-done.2.text_own = bf16[16,16,1152]{2,1,0:T(8,128)(2,1)S(1)} async-done(((bf16[16,16,1152]{2,1,0:T(8,128)(2,1)}), bf16[16,16,1152]{2,1,0:T(8,128)(2,1)S(1)}, u32[]{:S(2)}, u32[]{:S(2)}) %all-to-all-start.2) | async-done | bytes 589856 | tf_op jit(solution)/shard_map/all_to_all | solution.py:203
  62.4 6.2 %collective-permute-start.3 = (bf16[16,16,1152]{2,1,0:T(8,128)(2,1)S(1)}, bf16[16,16,1152]{2,1,0:T(8,128)(2,1)S(1)}, u32[]{:S(2)}, u32[]{:S(2)}) collective-permute-start(bf16[16,16,1152]{2,1,0:T(8,128)(2,1)S(1)} %all-to-all-done.2.text_own), channel_id=1, source_target_pairs={{0,4},{4,0},{1,5},{5,1},{2,6},{6,2},{3,7},{7,3},{8,12},{12,8},{9,1... | collective-permute-start | bytes 1769480 | tf_op jit(solution)/shard_map/ppermute | solution.py:44
  68.7 1.6 %collective-permute-done.3.text_other = bf16[16,16,1152]{2,1,0:T(8,128)(2,1)S(1)} collective-permute-done((bf16[16,16,1152]{2,1,0:T(8,128)(2,1)S(1)}, bf16[16,16,1152]{2,1,0:T(8,128)(2,1)S(1)}, u32[]{:S(2)}, u32[]{:S(2)}) %collective-permute-start.3) | collective-permute-done | bytes 589856 | tf_op jit(solution)/shard_map/ppermute | solution.py:44
  70.3 2.5 %shard_map.107 = bf16[16,2,16,1152]{3,2,1,0:T(8,128)(2,1)S(1)} custom-call(s32[3]{0:T(128)S(1)} %pad_add_fusion.place, f32[2]{0:T(128)S(1)} %pad_maximum_fusion.2.numbers, bf16[16,16,1152]{2,1,0:T(8,128)(2,1)S(1)} %all-to-all-done.2.text_own, bf16[16,16,1152]{2,1,0:T(8,128)(2,1)S(1)} %collective-permute-done.3.text_other, ...), custom_call_target="tpu_custom_call" | custom-call | flops 1200000000 | bytes 100000 | tf_op jit(solution)/shard_map/pallas_call | solution.py:32
  72.8 26.7 %all_to_all.21.parts = bf16[16,2,16,1152]{3,2,1,0:T(8,128)(2,1)S(1)} all-to-all(bf16[16,2,16,1152]{3,2,1,0:T(8,128)(2,1)S(1)} %shard_map.107), channel_id=1, replica_groups={{0,32,64,96,128,160,192,224,256,288,320,352,384,416,448,480},{1,33,65,9..., dimensions={0} | all-to-all | bytes 2359296 | tf_op jit(solution)/shard_map/all_to_all | solution.py:215
  99.6 0.2 shard_map.108
  99.7 2.1 %all-gather = f32[4,16,1152]{2,1,0:T(8,128)S(1)} all-gather(f32[2,16,1152]{2,1,0:T(8,128)S(1)} %shard_map.108), channel_id=2, replica_groups=mesh['yl'=2,'z'=8,'x'=4,'core'=2,'t'=4] {'core'}, dimensions={0}, use_global_device_ids=true | all-gather | bytes 442368 | tf_op jit(solution)/shard_map/all_gather | solution.py:217
  101.9 0.7 dynamic-slice_bitcast_fusion
  (3 shorter events, 0.1 us)
Async XLA Ops:
  2.1 15.7 %all-to-all-start = ((bf16[4,64,288]{2,1,0:T(8,128)(2,1)}), bf16[4,64,288]{2,1,0:T(8,128)(2,1)S(1)}, u32[]{:S(2)}, u32[]{:S(2)}) async-start(bf16[4,64,288]{2,1,0:T(8,128)(2,1)} %broadcast_in_dim.4), calls=%async_computation | async-start | bytes 393216 | tf_op jit(solution)/shard_map/all_to_all | solution.py:178
  11.1 0.9 copy-start
  12.2 8.2 %collective-permute-start = (bf16[64,1280]{1,0:T(8,128)(2,1)S(1)}, bf16[64,1280]{1,0:T(8,128)(2,1)S(1)}, u32[]{:S(2)}, u32[]{:S(2)}) collective-permute-start(bf16[64,1280]{1,0:T(8,128)(2,1)S(1)} %shard_map.105), channel_id=1, source_target_pairs={{0,16},{8,24},{16,0},{24,8},{1,17},{9,25},{17,1},{25,9},{2,18},{10... | collective-permute-start | bytes 491528 | tf_op jit(solution)/shard_map/ppermute | solution.py:48
  20.4 16.2 %collective-permute-start.1 = (bf16[128,1280]{1,0:T(8,128)(2,1)S(1)}, bf16[128,1280]{1,0:T(8,128)(2,1)S(1)}, u32[]{:S(2)}, u32[]{:S(2)}) collective-permute-start(bf16[128,1280]{1,0:T(8,128)(2,1)S(1)} %pad_maximum_fusion.1), channel_id=1, source_target_pairs={{0,8},{8,0},{16,24},{24,16},{1,9},{9,1},{17,25},{25,17},{2,10},{10... | collective-permute-start | bytes 983048 | tf_op jit(solution)/shard_map/ppermute | solution.py:48
  37.7 24.8 %all-to-all-start.2 = ((bf16[16,16,1152]{2,1,0:T(8,128)(2,1)}), bf16[16,16,1152]{2,1,0:T(8,128)(2,1)S(1)}, u32[]{:S(2)}, u32[]{:S(2)}) async-start(bf16[16,16,1152]{2,1,0:T(8,128)(2,1)} %shard_map.106), calls=%async_computation.2 | async-start | bytes 1179648 | tf_op jit(solution)/shard_map/all_to_all | solution.py:203
  48.5 8.2 %collective-permute-start.2 = (bf16[256,1280]{1,0:T(8,128)(2,1)S(1)}, bf16[256,1280]{1,0:T(8,128)(2,1)S(1)}, u32[]{:S(2)}, u32[]{:S(2)}) collective-permute-start(bf16[256,1280]{1,0:T(8,128)(2,1)S(1)} %pad_maximum_fusion.image_own), channel_id=1, source_target_pairs={{0,4},{4,0},{1,5},{5,1},{2,6},{6,2},{3,7},{7,3},{8,12},{12,8},{9,1... | collective-permute-start | bytes 1966088 | tf_op jit(solution)/shard_map/ppermute | solution.py:44
  62.4 7.9 %collective-permute-start.3 = (bf16[16,16,1152]{2,1,0:T(8,128)(2,1)S(1)}, bf16[16,16,1152]{2,1,0:T(8,128)(2,1)S(1)}, u32[]{:S(2)}, u32[]{:S(2)}) collective-permute-start(bf16[16,16,1152]{2,1,0:T(8,128)(2,1)S(1)} %all-to-all-done.2.text_own), channel_id=1, source_target_pairs={{0,4},{4,0},{1,5},{5,1},{2,6},{6,2},{3,7},{7,3},{8,12},{12,8},{9,1... | collective-permute-start | bytes 1769480 | tf_op jit(solution)/shard_map/ppermute | solution.py:44

commit v5 on v4

--- a/solution.py
+++ b/solution.py
@@ -103,57 +103,70 @@
         copies[k] = row
 
 
-def pair_kernel(place, numbers, text_own, text_other, image_own, image_other, out):
-    groups, _, own, width = out.shape
+def grad_shares(place, numbers, text, from_other, images, size):
+    groups, own, width = text.shape
     x, core, t = place[0], place[1], place[2]
     scale, shift = numbers[0], numbers[1]
-    ring, tensor = SIZES["x"], SIZES["t"]
-    block = tensor * own
+    block = SIZES["t"] * own
+    many = groups * own
     lane = lax.broadcasted_iota(jnp.int32, (8, LANES), 1)
     digit = jnp.where(lane == 0, float(LANES), jnp.where(lane == 1, 1.0, 0.0)).astype(BF16)
-
-    def ids(shape, dim, which):
+    text_core = (1 - core) if from_other else core
+    first = (x * 2 + text_core) * block + t * own
+
+    def ids(shape, dim):
         row = lax.broadcasted_iota(jnp.int32, shape, dim)
-        first = (x * 2 + which) * block + t * own
-        return ((row // own) * (ring * 2 * block) + first + row % own).astype(F32)
+        return ((row // own) * (SIZES["x"] * 2 * block) + first + row % own).astype(F32)
 
     def weights(a, b, match):
         scores = scale * nt(a, b) + shift
         score = jnp.where(match, -scores, scores)
-        size = jnp.where(match, -scale, scale)
-        return (size / (1.0 + jnp.exp(-score))).astype(BF16)
-
-    texts = ((text_own, core), (text_other, 1 - core))
-    images = ((image_own, core), (image_other, 1 - core))
-    many = groups * own
-
-    @pl.when(core == 0)
+        return (jnp.where(match, -scale, scale) / (1.0 + jnp.exp(-score))).astype(BF16)
+
+    rows = text[...].reshape(many, width)
+    if size == 1:
+        total = None
+        for image in images:
+            b = image[:, :width]
+            match = ids((many, 1), 0) == nt(digit, image[:, width:])[:1]
+            part = nn(weights(rows, b, match), b)
+            total = part if total is None else total + part
+        return [total]
+    shares = []
+    for image in images:
+        match = nt(image[:, width:], digit)[:, :1] == ids((1, many), 1)
+        shares.append(nn(weights(image[:, :width], rows, match), rows))
+    return shares
+
+
+def first_kernel(place, numbers, text, image_own, image_other, held):
+    for core in range(2):
+
+        @pl.when(place[1] == core)
+        def _():
+            shares = grad_shares(place, numbers, text, False, (image_own, image_other), core + 1)
+            for k, share in enumerate(shares):
+                held[k] = share
+
+
+def second_kernel(place, numbers, text, image_own, image_other, held, out):
+    groups, _, own, width = out.shape
+    tensor = SIZES["t"]
+    block = tensor * own
+
+    @pl.when(place[1] == 0)
     def _():
-        for which, (text, from_core) in enumerate(texts):
-            a = text[...].reshape(many, width)
-            total = None
-            for image, _ in images:
-                b = image[:, :width]
-                position = nt(digit, image[:, width:])[:1]
-                match = ids((many, 1), 0, from_core) == position
-                part = nn(weights(a, b, match), b)
-                total = part if total is None else total + part
-            out[:, which] = total.astype(BF16).reshape(groups, own, width)
-
-    @pl.when(core == 1)
+        shares = grad_shares(place, numbers, text, True, (image_own, image_other), 1)
+        out[:, 0] = held[0].astype(BF16).reshape(groups, own, width)
+        out[:, 1] = shares[0].astype(BF16).reshape(groups, own, width)
+
+    @pl.when(place[1] == 1)
     def _():
-        for which, (image, from_core) in enumerate(images):
-            a = image[:, :width]
-            position = nt(image[:, width:], digit)[:, :1]
-            total = None
-            for text, text_core in texts:
-                b = text[...].reshape(many, width)
-                match = position == ids((1, many), 1, text_core)
-                part = nn(weights(a, b, match), b)
-                total = part if total is None else total + part
-            total = total.astype(BF16)
+        shares = grad_shares(place, numbers, text, True, (image_own, image_other), 2)
+        for which, share in enumerate(shares):
+            total = (held[which] + share).astype(BF16)
             for k, bits in enumerate((0, 2, 1, 3)):
-                at = jnp.bitwise_xor(x, bits)
+                at = jnp.bitwise_xor(place[0], bits)
                 rows = total[k * block : (k + 1) * block].reshape(tensor, own, width)
                 out[pl.ds(at * tensor, tensor), 1 - which] = rows
 
@@ -190,27 +203,30 @@
         + [pltpu.SemaphoreType.DMA((2,))],
         room=FULL,
     )
-    partial, packed, moved = lax.optimization_barrier((partial, packed, moved))
+    parts = lax.all_to_all(partial, "t", 0, 0)
     couple = jnp.concatenate([packed, moved], axis=0)
-    partial, couple = lax.optimization_barrier((partial, couple))
+    copies = call(text_kernel, bf16((groups, own, width)), (parts,))
     moved = swap_along_x(couple, 1)
-    parts = lax.all_to_all(partial, "t", 0, 0)
-    parts, couple, moved = lax.optimization_barrier((parts, couple, moved))
     image_own = jnp.concatenate([couple, moved], axis=0)
-    copies = call(text_kernel, bf16((groups, own, width)), (parts,))
-    copies, image_own = lax.optimization_barrier((copies, image_own))
     image_other = swap_cores(image_own)
     text_own = lax.all_to_all(copies, ("yl", "z"), 0, 0)
-    text_own, image_other, place, numbers, core = lax.optimization_barrier(
-        (text_own, image_other, place, numbers, core)
+    text_own, image_own, image_other, place, numbers, core = lax.optimization_barrier(
+        (text_own, image_own, image_other, place, numbers, core)
     )
     text_other = swap_cores(text_own)
+    held = call(
+        first_kernel,
+        f32((2, groups * own, width)),
+        (place, numbers, text_own, image_own, image_other),
+        scalars=2,
+        flops=600_000_000,
+    )
     shares = call(
-        pair_kernel,
-        jax.ShapeDtypeStruct((groups, 2, own, width), BF16),
-        (place, numbers, text_own, text_other, image_own, image_other),
+        second_kernel,
+        bf16((groups, 2, own, width)),
+        (place, numbers, text_other, image_own, image_other, held),
         scalars=2,
-        flops=1_200_000_000,
+        flops=600_000_000,
     )
     shares = lax.all_to_all(shares, ALL, 0, 0, axis_index_groups=grad_groups())
     total = call(sum_kernel, f32((2, own, width)), (shares,))

time: 103 us -> 99.5 us (0.966)
  blocking collectives: 42.1 us -> 29.8 us
  waiting for transfers between devices: 8.63 us -> 12.7 us
  Pallas kernels: 6.3 us -> 8.61 us
  starting transfers between devices: 38.9 us -> 40.9 us
    all_to_all x1 -> x0, blocking collectives: 13.2 us -> none  [shards(): parts = lax.all_to_all(partial, 't', 0, 0)]
    all_to_all x0 -> x1, starting transfers between devices: none -> 5.65 us  [shards(): parts = lax.all_to_all(partial, 't', 0, 0)]
    all_to_all x0 -> x1, waiting for transfers between devices: none -> 5.09 us  [shards(): parts = lax.all_to_all(partial, 't', 0, 0)]
    ppermute x2, starting transfers between devices: 12.7 us -> 10.4 us  [swap_cores(): return lax.ppermute(block, 'core', [(0, 1), (1, 0)])]
    pallas_call x5 -> x6, Pallas kernels: 6.3 us -> 8.61 us  [call(): pl.pallas_call(kernel, out_shape=outs, in_specs=specs or [SMEM] * scalars...]
    ppermute x2, waiting for transfers between devices: 1.86 us -> 0.25 us  [swap_cores(): return lax.ppermute(block, 'core', [(0, 1), (1, 0)])]
  transfers between devices with their start and end apart: 6 -> 7, of which waited for: 4 -> 4; matrix products, arithmetic and copies ran while one was open for 1% -> 2% of each run, Pallas kernels for 3% -> 6%
where the time goes in v5:
time: 99.5 us; the launch traced here: 98.8 us
  starting transfers between devices  40.9 us (41%)
  blocking collectives  29.8 us (30%)
  waiting for transfers between devices  12.7 us (13%)
  Pallas kernels  8.61 us (9%)
  local copies, waits for them, and re-layouts  3.1 us (3%)
  between operations  2.03 us (2%)
  other arithmetic  1.59 us (2%)
    all_to_all x1, blocking collectives, shards(): shares = lax.all_to_all(shares, ALL, 0, 0, axis_index_groups=grad_groups())  26.8 us
    ppermute x2, starting transfers between devices, swap_cores(): return lax.ppermute(block, 'core', [(0, 1), (1, 0)])  10.4 us
    all_to_all x1, starting transfers between devices, shards(): text_own = lax.all_to_all(copies, ('yl', 'z'), 0, 0)  10.3 us
    pallas_call x6, Pallas kernels, call(): pl.pallas_call(kernel, out_shape=outs, in_specs=specs or [SMEM] * scalars...  8.61 us
    all_to_all x1, starting transfers between devices, shards(): gathered = lax.all_to_all(to_all, 't', 0, 0)  7.64 us
    ppermute x2, starting transfers between devices, swap_along_x(): lax.ppermute(block, 'x', [(i, i ^ bit) for i in range(lax.axis_size('x'))])  6.87 us
    all_to_all x1, waiting for transfers between devices, shards(): text_own = lax.all_to_all(copies, ('yl', 'z'), 0, 0)  6.38 us
    all_to_all x1, starting transfers between devices, shards(): parts = lax.all_to_all(partial, 't', 0, 0)  5.65 us
  transfers between devices with their start and end apart: 7, of which 4 were waited for; matrix products, arithmetic and copies ran while one was open for 2% of the time, Pallas kernels for 6%

profile of v5, /device:TPU:1, one launch (start us, length us, event | category | flops | bytes accessed | tf_op | source)
XLA Modules:
  0.0 98.8 jit_solution(13674897711504682382)
XLA Ops:
  0.6 1.5 %broadcast_in_dim.4 = bf16[4,64,288]{2,1,0:T(8,128)(2,1)} broadcast(bf16[64,288]{1,0:T(8,128)(2,1)} %param.9), dimensions={1,2} | broadcast | bytes 184320 | tf_op jit(solution)/shard_map/broadcast_in_dim | solution.py:190
  2.1 7.6 %all-to-all-start = ((bf16[4,64,288]{2,1,0:T(8,128)(2,1)}), bf16[4,64,288]{2,1,0:T(8,128)(2,1)S(1)}, u32[]{:S(2)}, u32[]{:S(2)}) async-start(bf16[4,64,288]{2,1,0:T(8,128)(2,1)} %broadcast_in_dim.4), calls=%async_computation | async-start | bytes 393216 | tf_op jit(solution)/shard_map/all_to_all | solution.py:191
  9.8 0.7 convert_element_type.5
  10.4 0.7 fusion
  11.1 0.0 copy-start
  11.1 0.9 copy-done
  12.0 0.1 shard_map.106
  12.2 4.7 %collective-permute-start = (bf16[64,1280]{1,0:T(8,128)(2,1)S(1)}, bf16[64,1280]{1,0:T(8,128)(2,1)S(1)}, u32[]{:S(2)}, u32[]{:S(2)}) collective-permute-start(bf16[64,1280]{1,0:T(8,128)(2,1)S(1)} %shard_map.106), channel_id=1, source_target_pairs={{0,16},{8,24},{16,0},{24,8},{1,17},{9,25},{17,1},{25,9},{2,18},{10... | collective-permute-start | bytes 491528 | tf_op jit(solution)/shard_map/ppermute | solution.py:48
  16.8 1.0 %all-to-all-done.gathered = bf16[4,64,288]{2,1,0:T(8,128)(2,1)S(1)} async-done(((bf16[4,64,288]{2,1,0:T(8,128)(2,1)}), bf16[4,64,288]{2,1,0:T(8,128)(2,1)S(1)}, u32[]{:S(2)}, u32[]{:S(2)}) %all-to-all-start) | async-done | bytes 147488 | tf_op jit(solution)/shard_map/all_to_all | solution.py:191
  17.9 3.2 %shard_map.104 = bf16[4,16,1152]{2,1,0:T(8,128)(2,1)} custom-call(bf16[4,64,288]{2,1,0:T(8,128)(2,1)S(1)} %all-to-all-done.gathered, f32[1,2048]{1,0:T(1,128)S(1)} %bitcast.9, bf16[1152,768]{1,0:T(8,128)(2,1)} %w1.1, bf16[768,1152]{1,0:T(8,128)(2,1)} %w2.1), custom_call_target="tpu_custom_call" | custom-call | bytes 100000 | tf_op jit(solution)/shard_map/pallas_call | solution.py:32
  21.1 5.6 %all-to-all-start.1 = ((bf16[4,16,1152]{2,1,0:T(8,128)(2,1)}), bf16[4,16,1152]{2,1,0:T(8,128)(2,1)S(1)}, u32[]{:S(2)}, u32[]{:S(2)}) async-start(bf16[4,16,1152]{2,1,0:T(8,128)(2,1)} %shard_map.104), calls=%async_computation.1 | async-start | bytes 294912 | tf_op jit(solution)/shard_map/all_to_all | solution.py:206
  26.7 0.0 collective-permute-done
  26.7 2.2 %collective-permute-start.1 = (bf16[128,1280]{1,0:T(8,128)(2,1)S(1)}, bf16[128,1280]{1,0:T(8,128)(2,1)S(1)}, u32[]{:S(2)}, u32[]{:S(2)}) collective-permute-start(bf16[128,1280]{1,0:T(8,128)(2,1)S(1)} %pad_maximum_fusion.1), channel_id=1, source_target_pairs={{0,8},{8,0},{16,24},{24,16},{1,9},{9,1},{17,25},{25,17},{2,10},{10... | collective-permute-start | bytes 983048 | tf_op jit(solution)/shard_map/ppermute | solution.py:48
  29.0 5.1 %all-to-all-done.1.parts = bf16[4,16,1152]{2,1,0:T(8,128)(2,1)S(1)} async-done(((bf16[4,16,1152]{2,1,0:T(8,128)(2,1)}), bf16[4,16,1152]{2,1,0:T(8,128)(2,1)S(1)}, u32[]{:S(2)}, u32[]{:S(2)}) %all-to-all-start.1) | async-done | bytes 147488 | tf_op jit(solution)/shard_map/all_to_all | solution.py:206
  34.1 1.0 shard_map.105
  35.0 10.3 %all-to-all-start.2 = ((bf16[16,16,1152]{2,1,0:T(8,128)(2,1)}), bf16[16,16,1152]{2,1,0:T(8,128)(2,1)S(1)}, u32[]{:S(2)}, u32[]{:S(2)}) async-start(bf16[16,16,1152]{2,1,0:T(8,128)(2,1)} %shard_map.105), calls=%async_computation.2 | async-start | bytes 1179648 | tf_op jit(solution)/shard_map/all_to_all | solution.py:212
  45.4 0.0 collective-permute-done.1
  45.4 5.4 %collective-permute-start.2 = (bf16[256,1280]{1,0:T(8,128)(2,1)S(1)}, bf16[256,1280]{1,0:T(8,128)(2,1)S(1)}, u32[]{:S(2)}, u32[]{:S(2)}) collective-permute-start(bf16[256,1280]{1,0:T(8,128)(2,1)S(1)} %pad_maximum_fusion.image_own), channel_id=1, source_target_pairs={{0,4},{4,0},{1,5},{5,1},{2,6},{6,2},{3,7},{7,3},{8,12},{12,8},{9,1... | collective-permute-start | bytes 1966088 | tf_op jit(solution)/shard_map/ppermute | solution.py:44
  52.2 0.1 pad_maximum_fusion.2.numbers
  52.3 0.1 pad_add_fusion.place
  52.3 0.3 collective-permute-done.2.image_other
  52.6 6.4 %all-to-all-done.2.text = bf16[16,16,1152]{2,1,0:T(8,128)(2,1)S(1)} async-done(((bf16[16,16,1152]{2,1,0:T(8,128)(2,1)}), bf16[16,16,1152]{2,1,0:T(8,128)(2,1)S(1)}, u32[]{:S(2)}, u32[]{:S(2)}) %all-to-all-start.2) | async-done | bytes 589856 | tf_op jit(solution)/shard_map/all_to_all | solution.py:212
  59.0 4.9 %collective-permute-start.3 = (bf16[16,16,1152]{2,1,0:T(8,128)(2,1)S(1)}, bf16[16,16,1152]{2,1,0:T(8,128)(2,1)S(1)}, u32[]{:S(2)}, u32[]{:S(2)}) collective-permute-start(bf16[16,16,1152]{2,1,0:T(8,128)(2,1)S(1)} %all-to-all-done.2.text), channel_id=1, source_target_pairs={{0,4},{4,0},{1,5},{5,1},{2,6},{6,2},{3,7},{7,3},{8,12},{12,8},{9,1... | collective-permute-start | bytes 1769480 | tf_op jit(solution)/shard_map/ppermute | solution.py:44
  63.9 2.1 %shard_map.107.held = f32[2,256,1152]{2,1,0:T(8,128)S(1)} custom-call(s32[3]{0:T(128)S(1)} %pad_add_fusion.place, f32[2]{0:T(128)S(1)} %pad_maximum_fusion.2.numbers, bf16[16,16,1152]{2,1,0:T(8,128)(2,1)S(1)} %all-to-all-done.2.text, bf16[256,1280]{1,0:T(8,128)(2,1)S(1)} %pad_maximum_fusion.image_own, bf16[256,1280]{1,0:T(8,128)(2,1)S(1)} %collective-permute-done.2.image_other), custom_call_target="tpu_custom_call" | custom-call | flops 600000000 | bytes 100000 | tf_op jit(solution)/shard_map/pallas_call | solution.py:32
  66.0 0.0 collective-permute-done.3.text
  66.0 2.1 %shard_map.108 = bf16[16,2,16,1152]{3,2,1,0:T(8,128)(2,1)S(1)} custom-call(s32[3]{0:T(128)S(1)} %pad_add_fusion.place, f32[2]{0:T(128)S(1)} %pad_maximum_fusion.2.numbers, bf16[16,16,1152]{2,1,0:T(8,128)(2,1)S(1)} %collective-permute-done.3.text, bf16[256,1280]{1,0:T(8,128)(2,1)S(1)} %pad_maximum_fusion.image_own, ...), custom_call_target="tpu_custom_call" | custom-call | flops 600000000 | bytes 100000 | tf_op jit(solution)/shard_map/pallas_call | solution.py:32
  68.1 26.8 %all_to_all.20.parts = bf16[16,2,16,1152]{3,2,1,0:T(8,128)(2,1)S(1)} all-to-all(bf16[16,2,16,1152]{3,2,1,0:T(8,128)(2,1)S(1)} %shard_map.108), channel_id=1, replica_groups={{0,32,64,96,128,160,192,224,256,288,320,352,384,416,448,480},{1,33,65,9..., dimensions={0} | all-to-all | bytes 2359296 | tf_op jit(solution)/shard_map/all_to_all | solution.py:231
  94.9 0.2 shard_map.109
  95.1 3.0 %all-gather = f32[4,16,1152]{2,1,0:T(8,128)S(1)} all-gather(f32[2,16,1152]{2,1,0:T(8,128)S(1)} %shard_map.109), channel_id=2, replica_groups=mesh['yl'=2,'z'=8,'x'=4,'core'=2,'t'=4] {'core'}, dimensions={0}, use_global_device_ids=true | all-gather | bytes 442368 | tf_op jit(solution)/shard_map/all_gather | solution.py:233
  98.1 0.7 dynamic-slice_bitcast_fusion
  (3 shorter events, 0.1 us)
Async XLA Ops:
  2.1 15.7 %all-to-all-start = ((bf16[4,64,288]{2,1,0:T(8,128)(2,1)}), bf16[4,64,288]{2,1,0:T(8,128)(2,1)S(1)}, u32[]{:S(2)}, u32[]{:S(2)}) async-start(bf16[4,64,288]{2,1,0:T(8,128)(2,1)} %broadcast_in_dim.4), calls=%async_computation | async-start | bytes 393216 | tf_op jit(solution)/shard_map/all_to_all | solution.py:191
  11.1 0.9 copy-start
  12.2 14.5 %collective-permute-start = (bf16[64,1280]{1,0:T(8,128)(2,1)S(1)}, bf16[64,1280]{1,0:T(8,128)(2,1)S(1)}, u32[]{:S(2)}, u32[]{:S(2)}) collective-permute-start(bf16[64,1280]{1,0:T(8,128)(2,1)S(1)} %shard_map.106), channel_id=1, source_target_pairs={{0,16},{8,24},{16,0},{24,8},{1,17},{9,25},{17,1},{25,9},{2,18},{10... | collective-permute-start | bytes 491528 | tf_op jit(solution)/shard_map/ppermute | solution.py:48
  21.1 13.0 %all-to-all-start.1 = ((bf16[4,16,1152]{2,1,0:T(8,128)(2,1)}), bf16[4,16,1152]{2,1,0:T(8,128)(2,1)S(1)}, u32[]{:S(2)}, u32[]{:S(2)}) async-start(bf16[4,16,1152]{2,1,0:T(8,128)(2,1)} %shard_map.104), calls=%async_computation.1 | async-start | bytes 294912 | tf_op jit(solution)/shard_map/all_to_all | solution.py:206
  26.7 18.6 %collective-permute-start.1 = (bf16[128,1280]{1,0:T(8,128)(2,1)S(1)}, bf16[128,1280]{1,0:T(8,128)(2,1)S(1)}, u32[]{:S(2)}, u32[]{:S(2)}) collective-permute-start(bf16[128,1280]{1,0:T(8,128)(2,1)S(1)} %pad_maximum_fusion.1), channel_id=1, source_target_pairs={{0,8},{8,0},{16,24},{24,16},{1,9},{9,1},{17,25},{25,17},{2,10},{10... | collective-permute-start | bytes 983048 | tf_op jit(solution)/shard_map/ppermute | solution.py:48
  35.0 23.9 %all-to-all-start.2 = ((bf16[16,16,1152]{2,1,0:T(8,128)(2,1)}), bf16[16,16,1152]{2,1,0:T(8,128)(2,1)S(1)}, u32[]{:S(2)}, u32[]{:S(2)}) async-start(bf16[16,16,1152]{2,1,0:T(8,128)(2,1)} %shard_map.105), calls=%async_computation.2 | async-start | bytes 1179648 | tf_op jit(solution)/shard_map/all_to_all | solution.py:212
  45.4 7.2 %collective-permute-start.2 = (bf16[256,1280]{1,0:T(8,128)(2,1)S(1)}, bf16[256,1280]{1,0:T(8,128)(2,1)S(1)}, u32[]{:S(2)}, u32[]{:S(2)}) collective-permute-start(bf16[256,1280]{1,0:T(8,128)(2,1)S(1)} %pad_maximum_fusion.image_own), channel_id=1, source_target_pairs={{0,4},{4,0},{1,5},{5,1},{2,6},{6,2},{3,7},{7,3},{8,12},{12,8},{9,1... | collective-permute-start | bytes 1966088 | tf_op jit(solution)/shard_map/ppermute | solution.py:44
  59.0 7.0 %collective-permute-start.3 = (bf16[16,16,1152]{2,1,0:T(8,128)(2,1)S(1)}, bf16[16,16,1152]{2,1,0:T(8,128)(2,1)S(1)}, u32[]{:S(2)}, u32[]{:S(2)}) collective-permute-start(bf16[16,16,1152]{2,1,0:T(8,128)(2,1)S(1)} %all-to-all-done.2.text), channel_id=1, source_target_pairs={{0,4},{4,0},{1,5},{5,1},{2,6},{6,2},{3,7},{7,3},{8,12},{12,8},{9,1... | collective-permute-start | bytes 1769480 | tf_op jit(solution)/shard_map/ppermute | solution.py:44

commit v6 on v5

--- a/solution.py
+++ b/solution.py
@@ -1,4 +1,5 @@
 import functools
+import itertools
 
 import jax
 import jax.numpy as jnp
@@ -8,9 +9,11 @@
 from jax.sharding import Mesh, PartitionSpec as P
 
 EPSILON = 1e-06
-ROWS = ("yl", "z", "x", "core")
+ROWS = ("yl", "z", "xh", "xl", "core")
 ALL = ROWS + ("t",)
-SIZES = dict(yl=2, z=8, x=4, core=2, t=4)
+SIZES = dict(yl=2, z=8, xh=2, xl=2, core=2, t=4)
+TEXT_GROUP = ("z", "xl")
+IMAGE_GROUP = ("yl", "xh", "t")
 BF16 = jnp.bfloat16
 F32 = jnp.float32
 LANES = 128
@@ -40,23 +43,26 @@
     )(*operands)
 
 
-def swap_cores(block):
-    return lax.ppermute(block, "core", [(0, 1), (1, 0)])
-
-
-def swap_along_x(block, bit):
-    return lax.ppermute(block, "x", [(i, i ^ bit) for i in range(lax.axis_size("x"))])
+def swap(block, axis):
+    return lax.ppermute(block, axis, [(0, 1), (1, 0)])
 
 
 def grad_groups():
-    yl, z, x, core, t = (SIZES[a] for a in ALL)
-
-    def flat(i, j, k, c, m):
-        return (((i * z + j) * x + k) * core + c) * t + m
-
-    text = [[flat(i, j, k, 0, m) for i in range(yl) for j in range(z)] for k in range(x) for m in range(t)]
-    image = [[flat(i, j, k, 1, m) for k in range(x) for m in range(t)] for i in range(yl) for j in range(z)]
-    return text + image
+    def groups(core, inside):
+        outside = [a for a in ALL if a not in inside and a != "core"]
+        out = []
+        for fixed in itertools.product(*(range(SIZES[a]) for a in outside)):
+            group = []
+            for moving in itertools.product(*(range(SIZES[a]) for a in inside)):
+                at = dict(zip(outside, fixed), **dict(zip(inside, moving)), core=core)
+                number = 0
+                for a in ALL:
+                    number = number * SIZES[a] + at[a]
+                group.append(number)
+            out.append(group)
+        return out
+
+    return groups(0, TEXT_GROUP) + groups(1, IMAGE_GROUP)
 
 
 def unit(values):
@@ -105,18 +111,20 @@
 
 def grad_shares(place, numbers, text, from_other, images, size):
     groups, own, width = text.shape
-    x, core, t = place[0], place[1], place[2]
+    yl, core, t, xbit = place[0], place[1], place[2], place[3]
     scale, shift = numbers[0], numbers[1]
     block = SIZES["t"] * own
     many = groups * own
     lane = lax.broadcasted_iota(jnp.int32, (8, LANES), 1)
     digit = jnp.where(lane == 0, float(LANES), jnp.where(lane == 1, 1.0, 0.0)).astype(BF16)
     text_core = (1 - core) if from_other else core
-    first = (x * 2 + text_core) * block + t * own
+    chip_row = 8 * block
+    first = yl * (SIZES["z"] * chip_row) + (xbit * 4 + text_core) * block + t * own
 
     def ids(shape, dim):
         row = lax.broadcasted_iota(jnp.int32, shape, dim)
-        return ((row // own) * (SIZES["x"] * 2 * block) + first + row % own).astype(F32)
+        member = row // own
+        return ((member // 2) * chip_row + (member % 2) * (2 * block) + first + row % own).astype(F32)
 
     def weights(a, b, match):
         scores = scale * nt(a, b) + shift
@@ -165,8 +173,8 @@
         shares = grad_shares(place, numbers, text, True, (image_own, image_other), 2)
         for which, share in enumerate(shares):
             total = (held[which] + share).astype(BF16)
-            for k, bits in enumerate((0, 2, 1, 3)):
-                at = jnp.bitwise_xor(place[0], bits)
+            for k in range(4):
+                at = jnp.bitwise_xor(place[0], k % 2) * 2 + jnp.bitwise_xor(place[3], k // 2)
                 rows = total[k * block : (k + 1) * block].reshape(tensor, own, width)
                 out[pl.ds(at * tensor, tensor), 1 - which] = rows
 
@@ -179,12 +187,13 @@
 
 
 def shards(tokens, w1, b1, w2, b2, pictures, matching, sharpness, offset):
-    x, core, t = (lax.axis_index(a).astype(jnp.int32) for a in ("x", "core", "t"))
-    place = jnp.stack([x, core, t])
+    axes = ("yl", "core", "t", IMAGE_GROUP[1])
+    yl, core, t, xbit = (lax.axis_index(a).astype(jnp.int32) for a in axes)
+    place = jnp.stack([yl, core, t, xbit])
     rows, width = pictures.shape
     tensor = lax.axis_size("t")
     own = rows // tensor
-    groups = lax.axis_size(("yl", "z"))
+    groups = lax.axis_size(TEXT_GROUP)
 
     bf16, f32 = (functools.partial(jax.ShapeDtypeStruct, dtype=d) for d in (BF16, F32))
     to_all = jnp.broadcast_to(tokens[None], (tensor,) + tokens.shape)
@@ -192,7 +201,7 @@
     spots = jnp.pad(matching.astype(F32), (0, LANES - rows))
     small = jnp.concatenate([spots, b1, b2])[None]
     packed = call(pack_kernel, bf16((rows, width + LANES)), (pictures, small))
-    moved = swap_along_x(packed, 2)
+    moved = swap(packed, "yl")
     numbers = jnp.concatenate([sharpness, offset])
     partial = call(
         ffn_kernel,
@@ -206,14 +215,14 @@
     parts = lax.all_to_all(partial, "t", 0, 0)
     couple = jnp.concatenate([packed, moved], axis=0)
     copies = call(text_kernel, bf16((groups, own, width)), (parts,))
-    moved = swap_along_x(couple, 1)
+    moved = swap(couple, IMAGE_GROUP[1])
     image_own = jnp.concatenate([couple, moved], axis=0)
-    image_other = swap_cores(image_own)
-    text_own = lax.all_to_all(copies, ("yl", "z"), 0, 0)
+    image_other = swap(image_own, "core")
+    text_own = lax.all_to_all(copies, TEXT_GROUP, 0, 0)
     text_own, image_own, image_other, place, numbers, core = lax.optimization_barrier(
         (text_own, image_own, image_other, place, numbers, core)
     )
-    text_other = swap_cores(text_own)
+    text_other = swap(text_own, "core")
     held = call(
         first_kernel,
         f32((2, groups * own, width)),

time: 99.5 us -> 98.7 us (level)
  blocking collectives: 29.8 us -> 27.4 us
  starting transfers between devices: 40.9 us -> 42.1 us
    all_to_all x1, waiting for transfers between devices: 5.09 us -> 2.47 us  [shards(): parts = lax.all_to_all(partial, 't', 0, 0)]
    ppermute x4, starting transfers between devices: 17.3 us -> 19.7 us  [swap(): return lax.ppermute(block, axis, [(0, 1), (1, 0)])]
    all_to_all x1, waiting for transfers between devices: 1.02 us -> 3.36 us  [shards(): gathered = lax.all_to_all(to_all, 't', 0, 0)]
    all_to_all x1, starting transfers between devices: 5.65 us -> 3.37 us  [shards(): parts = lax.all_to_all(partial, 't', 0, 0)]
    all_to_all x1, blocking collectives: 26.8 us -> 25.3 us  [shards(): shares = lax.all_to_all(shares, ALL, 0, 0, axis_index_groups=grad_groups())]
    all_gather x1, blocking collectives: 3.02 us -> 2.02 us  [shards(): both = lax.all_gather(total, 'core')]
    all_to_all x1, starting transfers between devices: 10.3 us -> 11.3 us  [shards(): text_own = lax.all_to_all(copies, TEXT_GROUP, 0, 0)]
where the time goes in v6:
time: 98.7 us; the launch traced here: 98 us
  starting transfers between devices  42.1 us (43%)
  blocking collectives  27.4 us (28%)
  waiting for transfers between devices  13.2 us (13%)
  Pallas kernels  8.61 us (9%)
  local copies, waits for them, and re-layouts  3.1 us (3%)
  between operations  2.03 us (2%)
  other arithmetic  1.59 us (2%)
    all_to_all x1, blocking collectives, shards(): shares = lax.all_to_all(shares, ALL, 0, 0, axis_index_groups=grad_groups())  25.3 us
    ppermute x4, starting transfers between devices, swap(): return lax.ppermute(block, axis, [(0, 1), (1, 0)])  19.7 us
    all_to_all x1, starting transfers between devices, shards(): text_own = lax.all_to_all(copies, TEXT_GROUP, 0, 0)  11.3 us
    pallas_call x6, Pallas kernels, call(): pl.pallas_call(kernel, out_shape=outs, in_specs=specs or [SMEM] * scalars...  8.61 us
    all_to_all x1, starting transfers between devices, shards(): gathered = lax.all_to_all(to_all, 't', 0, 0)  7.64 us
    all_to_all x1, waiting for transfers between devices, shards(): text_own = lax.all_to_all(copies, TEXT_GROUP, 0, 0)  7.16 us
    all_to_all x1, starting transfers between devices, shards(): parts = lax.all_to_all(partial, 't', 0, 0)  3.37 us
    all_to_all x1, waiting for transfers between devices, shards(): gathered = lax.all_to_all(to_all, 't', 0, 0)  3.36 us
  transfers between devices with their start and end apart: 7, of which 4 were waited for; matrix products, arithmetic and copies ran while one was open for 2% of the time, Pallas kernels for 6%

profile of v6, /device:TPU:1, one launch (start us, length us, event | category | flops | bytes accessed | tf_op | source)
XLA Modules:
  0.0 98.0 jit_solution(14858094259099360423)
XLA Ops:
  0.6 1.5 %broadcast_in_dim.4 = bf16[4,64,288]{2,1,0:T(8,128)(2,1)} broadcast(bf16[64,288]{1,0:T(8,128)(2,1)} %param.9), dimensions={1,2} | broadcast | bytes 184320 | tf_op jit(solution)/shard_map/broadcast_in_dim | solution.py:199
  2.1 7.6 %all-to-all-start = ((bf16[4,64,288]{2,1,0:T(8,128)(2,1)}), bf16[4,64,288]{2,1,0:T(8,128)(2,1)S(1)}, u32[]{:S(2)}, u32[]{:S(2)}) async-start(bf16[4,64,288]{2,1,0:T(8,128)(2,1)} %broadcast_in_dim.4), calls=%async_computation | async-start | bytes 393216 | tf_op jit(solution)/shard_map/all_to_all | solution.py:200
  9.8 0.7 convert_element_type.5
  10.4 0.7 fusion
  11.1 0.0 copy-start
  11.1 0.9 copy-done
  12.0 0.1 shard_map.106
  12.2 2.3 %collective-permute-start = (bf16[64,1280]{1,0:T(8,128)(2,1)S(1)}, bf16[64,1280]{1,0:T(8,128)(2,1)S(1)}, u32[]{:S(2)}, u32[]{:S(2)}) collective-permute-start(bf16[64,1280]{1,0:T(8,128)(2,1)S(1)} %shard_map.106), channel_id=1, source_target_pairs={{0,256},{256,0},{1,257},{257,1},{2,258},{258,2},{3,259},{259,3},{4... | collective-permute-start | bytes 491528 | tf_op jit(solution)/shard_map/ppermute | solution.py:47
  14.5 3.4 %all-to-all-done.gathered = bf16[4,64,288]{2,1,0:T(8,128)(2,1)S(1)} async-done(((bf16[4,64,288]{2,1,0:T(8,128)(2,1)}), bf16[4,64,288]{2,1,0:T(8,128)(2,1)S(1)}, u32[]{:S(2)}, u32[]{:S(2)}) %all-to-all-start) | async-done | bytes 147488 | tf_op jit(solution)/shard_map/all_to_all | solution.py:200
  17.9 3.2 %shard_map.104 = bf16[4,16,1152]{2,1,0:T(8,128)(2,1)} custom-call(bf16[4,64,288]{2,1,0:T(8,128)(2,1)S(1)} %all-to-all-done.gathered, f32[1,2048]{1,0:T(1,128)S(1)} %bitcast.10, bf16[1152,768]{1,0:T(8,128)(2,1)} %w1.1, bf16[768,1152]{1,0:T(8,128)(2,1)} %w2.1), custom_call_target="tpu_custom_call" | custom-call | bytes 100000 | tf_op jit(solution)/shard_map/pallas_call | solution.py:35
  21.1 3.4 %all-to-all-start.1 = ((bf16[4,16,1152]{2,1,0:T(8,128)(2,1)}), bf16[4,16,1152]{2,1,0:T(8,128)(2,1)S(1)}, u32[]{:S(2)}, u32[]{:S(2)}) async-start(bf16[4,16,1152]{2,1,0:T(8,128)(2,1)} %shard_map.104), calls=%async_computation.1 | async-start | bytes 294912 | tf_op jit(solution)/shard_map/all_to_all | solution.py:215
  24.4 0.0 collective-permute-done
  24.5 4.9 %collective-permute-start.1 = (bf16[128,1280]{1,0:T(8,128)(2,1)S(1)}, bf16[128,1280]{1,0:T(8,128)(2,1)S(1)}, u32[]{:S(2)}, u32[]{:S(2)}) collective-permute-start(bf16[128,1280]{1,0:T(8,128)(2,1)S(1)} %pad_maximum_fusion.1), channel_id=1, source_target_pairs={{0,16},{16,0},{1,17},{17,1},{2,18},{18,2},{3,19},{19,3},{4,20},{20... | collective-permute-start | bytes 983048 | tf_op jit(solution)/shard_map/ppermute | solution.py:47
  29.4 2.5 %all-to-all-done.1.parts = bf16[4,16,1152]{2,1,0:T(8,128)(2,1)S(1)} async-done(((bf16[4,16,1152]{2,1,0:T(8,128)(2,1)}), bf16[4,16,1152]{2,1,0:T(8,128)(2,1)S(1)}, u32[]{:S(2)}, u32[]{:S(2)}) %all-to-all-start.1) | async-done | bytes 147488 | tf_op jit(solution)/shard_map/all_to_all | solution.py:215
  31.9 1.0 shard_map.105
  32.8 11.3 %all-to-all-start.2 = ((bf16[16,16,1152]{2,1,0:T(8,128)(2,1)}), bf16[16,16,1152]{2,1,0:T(8,128)(2,1)S(1)}, u32[]{:S(2)}, u32[]{:S(2)}) async-start(bf16[16,16,1152]{2,1,0:T(8,128)(2,1)} %shard_map.105), calls=%async_computation.2 | async-start | bytes 1179648 | tf_op jit(solution)/shard_map/all_to_all | solution.py:221
  44.2 0.0 collective-permute-done.1
  44.2 5.3 %collective-permute-start.2 = (bf16[256,1280]{1,0:T(8,128)(2,1)S(1)}, bf16[256,1280]{1,0:T(8,128)(2,1)S(1)}, u32[]{:S(2)}, u32[]{:S(2)}) collective-permute-start(bf16[256,1280]{1,0:T(8,128)(2,1)S(1)} %pad_maximum_fusion.image_own), channel_id=1, source_target_pairs={{0,4},{4,0},{1,5},{5,1},{2,6},{6,2},{3,7},{7,3},{8,12},{12,8},{9,1... | collective-permute-start | bytes 1966088 | tf_op jit(solution)/shard_map/ppermute | solution.py:47
  50.8 0.1 pad_maximum_fusion.2.numbers
  50.9 0.1 pad_add_fusion.place
  51.0 0.2 collective-permute-done.2.image_other
  51.2 7.2 %all-to-all-done.2.text = bf16[16,16,1152]{2,1,0:T(8,128)(2,1)S(1)} async-done(((bf16[16,16,1152]{2,1,0:T(8,128)(2,1)}), bf16[16,16,1152]{2,1,0:T(8,128)(2,1)S(1)}, u32[]{:S(2)}, u32[]{:S(2)}) %all-to-all-start.2) | async-done | bytes 589856 | tf_op jit(solution)/shard_map/all_to_all | solution.py:221
  58.4 7.2 %collective-permute-start.3 = (bf16[16,16,1152]{2,1,0:T(8,128)(2,1)S(1)}, bf16[16,16,1152]{2,1,0:T(8,128)(2,1)S(1)}, u32[]{:S(2)}, u32[]{:S(2)}) collective-permute-start(bf16[16,16,1152]{2,1,0:T(8,128)(2,1)S(1)} %all-to-all-done.2.text), channel_id=1, source_target_pairs={{0,4},{4,0},{1,5},{5,1},{2,6},{6,2},{3,7},{7,3},{8,12},{12,8},{9,1... | collective-permute-start | bytes 1769480 | tf_op jit(solution)/shard_map/ppermute | solution.py:47
  65.6 2.1 %shard_map.107.held = f32[2,256,1152]{2,1,0:T(8,128)S(1)} custom-call(s32[4]{0:T(128)S(1)} %pad_add_fusion.place, f32[2]{0:T(128)S(1)} %pad_maximum_fusion.2.numbers, bf16[16,16,1152]{2,1,0:T(8,128)(2,1)S(1)} %all-to-all-done.2.text, bf16[256,1280]{1,0:T(8,128)(2,1)S(1)} %pad_maximum_fusion.image_own, bf16[256,1280]{1,0:T(8,128)(2,1)S(1)} %collective-permute-done.2.image_other), custom_call_target="tpu_custom_call" | custom-call | flops 600000000 | bytes 100000 | tf_op jit(solution)/shard_map/pallas_call | solution.py:35
  67.7 0.0 collective-permute-done.3.text
  67.7 2.1 %shard_map.108 = bf16[16,2,16,1152]{3,2,1,0:T(8,128)(2,1)S(1)} custom-call(s32[4]{0:T(128)S(1)} %pad_add_fusion.place, f32[2]{0:T(128)S(1)} %pad_maximum_fusion.2.numbers, bf16[16,16,1152]{2,1,0:T(8,128)(2,1)S(1)} %collective-permute-done.3.text, bf16[256,1280]{1,0:T(8,128)(2,1)S(1)} %pad_maximum_fusion.image_own, ...), custom_call_target="tpu_custom_call" | custom-call | flops 600000000 | bytes 100000 | tf_op jit(solution)/shard_map/pallas_call | solution.py:35
  69.8 25.3 %all_to_all.20.parts = bf16[16,2,16,1152]{3,2,1,0:T(8,128)(2,1)S(1)} all-to-all(bf16[16,2,16,1152]{3,2,1,0:T(8,128)(2,1)S(1)} %shard_map.108), channel_id=1, replica_groups={{0,8,32,40,64,72,96,104,128,136,160,168,192,200,224,232},{1,9,33,41,65,..., dimensions={0} | all-to-all | bytes 2359296 | tf_op jit(solution)/shard_map/all_to_all | solution.py:240
  95.1 0.2 shard_map.109
  95.3 2.0 %all-gather = f32[4,16,1152]{2,1,0:T(8,128)S(1)} all-gather(f32[2,16,1152]{2,1,0:T(8,128)S(1)} %shard_map.109), channel_id=2, replica_groups=mesh['yl'=2,'z'=8,'xh'=2,'xl'=2,'core'=2,'t'=4] {'core'}, dimensions={0}, use_global_device_ids=true | all-gather | bytes 442368 | tf_op jit(solution)/shard_map/all_gather | solution.py:242
  97.3 0.7 dynamic-slice_bitcast_fusion
  (3 shorter events, 0.1 us)
Async XLA Ops:
  2.1 15.7 %all-to-all-start = ((bf16[4,64,288]{2,1,0:T(8,128)(2,1)}), bf16[4,64,288]{2,1,0:T(8,128)(2,1)S(1)}, u32[]{:S(2)}, u32[]{:S(2)}) async-start(bf16[4,64,288]{2,1,0:T(8,128)(2,1)} %broadcast_in_dim.4), calls=%async_computation | async-start | bytes 393216 | tf_op jit(solution)/shard_map/all_to_all | solution.py:200
  11.1 0.9 copy-start
  12.2 12.3 %collective-permute-start = (bf16[64,1280]{1,0:T(8,128)(2,1)S(1)}, bf16[64,1280]{1,0:T(8,128)(2,1)S(1)}, u32[]{:S(2)}, u32[]{:S(2)}) collective-permute-start(bf16[64,1280]{1,0:T(8,128)(2,1)S(1)} %shard_map.106), channel_id=1, source_target_pairs={{0,256},{256,0},{1,257},{257,1},{2,258},{258,2},{3,259},{259,3},{4... | collective-permute-start | bytes 491528 | tf_op jit(solution)/shard_map/ppermute | solution.py:47
  21.1 10.8 %all-to-all-start.1 = ((bf16[4,16,1152]{2,1,0:T(8,128)(2,1)}), bf16[4,16,1152]{2,1,0:T(8,128)(2,1)S(1)}, u32[]{:S(2)}, u32[]{:S(2)}) async-start(bf16[4,16,1152]{2,1,0:T(8,128)(2,1)} %shard_map.104), calls=%async_computation.1 | async-start | bytes 294912 | tf_op jit(solution)/shard_map/all_to_all | solution.py:215
  24.5 19.7 %collective-permute-start.1 = (bf16[128,1280]{1,0:T(8,128)(2,1)S(1)}, bf16[128,1280]{1,0:T(8,128)(2,1)S(1)}, u32[]{:S(2)}, u32[]{:S(2)}) collective-permute-start(bf16[128,1280]{1,0:T(8,128)(2,1)S(1)} %pad_maximum_fusion.1), channel_id=1, source_target_pairs={{0,16},{16,0},{1,17},{17,1},{2,18},{18,2},{3,19},{19,3},{4,20},{20... | collective-permute-start | bytes 983048 | tf_op jit(solution)/shard_map/ppermute | solution.py:47
  32.8 25.6 %all-to-all-start.2 = ((bf16[16,16,1152]{2,1,0:T(8,128)(2,1)}), bf16[16,16,1152]{2,1,0:T(8,128)(2,1)S(1)}, u32[]{:S(2)}, u32[]{:S(2)}) async-start(bf16[16,16,1152]{2,1,0:T(8,128)(2,1)} %shard_map.105), calls=%async_computation.2 | async-start | bytes 1179648 | tf_op jit(solution)/shard_map/all_to_all | solution.py:221
  44.2 7.0 %collective-permute-start.2 = (bf16[256,1280]{1,0:T(8,128)(2,1)S(1)}, bf16[256,1280]{1,0:T(8,128)(2,1)S(1)}, u32[]{:S(2)}, u32[]{:S(2)}) collective-permute-start(bf16[256,1280]{1,0:T(8,128)(2,1)S(1)} %pad_maximum_fusion.image_own), channel_id=1, source_target_pairs={{0,4},{4,0},{1,5},{5,1},{2,6},{6,2},{3,7},{7,3},{8,12},{12,8},{9,1... | collective-permute-start | bytes 1966088 | tf_op jit(solution)/shard_map/ppermute | solution.py:47
  58.4 9.3 %collective-permute-start.3 = (bf16[16,16,1152]{2,1,0:T(8,128)(2,1)S(1)}, bf16[16,16,1152]{2,1,0:T(8,128)(2,1)S(1)}, u32[]{:S(2)}, u32[]{:S(2)}) collective-permute-start(bf16[16,16,1152]{2,1,0:T(8,128)(2,1)S(1)} %all-to-all-done.2.text), channel_id=1, source_target_pairs={{0,4},{4,0},{1,5},{5,1},{2,6},{6,2},{3,7},{7,3},{8,12},{12,8},{9,1... | collective-permute-start | bytes 1769480 | tf_op jit(solution)/shard_map/ppermute | solution.py:47

commit v7 on v6

--- a/solution.py
+++ b/solution.py
@@ -12,8 +12,8 @@
 ROWS = ("yl", "z", "xh", "xl", "core")
 ALL = ROWS + ("t",)
 SIZES = dict(yl=2, z=8, xh=2, xl=2, core=2, t=4)
-TEXT_GROUP = ("z", "xl")
-IMAGE_GROUP = ("yl", "xh", "t")
+TEXT_GROUP = ("xl", "z")
+IMAGE_GROUP = ("xh", "yl", "t")
 BF16 = jnp.bfloat16
 F32 = jnp.float32
 LANES = 128
@@ -124,7 +124,8 @@
     def ids(shape, dim):
         row = lax.broadcasted_iota(jnp.int32, shape, dim)
         member = row // own
-        return ((member // 2) * chip_row + (member % 2) * (2 * block) + first + row % own).astype(F32)
+        xl, z = member // SIZES["z"], member % SIZES["z"]
+        return (z * chip_row + xl * (2 * block) + first + row % own).astype(F32)
 
     def weights(a, b, match):
         scores = scale * nt(a, b) + shift
@@ -174,7 +175,7 @@
         for which, share in enumerate(shares):
             total = (held[which] + share).astype(BF16)
             for k in range(4):
-                at = jnp.bitwise_xor(place[0], k % 2) * 2 + jnp.bitwise_xor(place[3], k // 2)
+                at = jnp.bitwise_xor(place[3], k // 2) * 2 + jnp.bitwise_xor(place[0], k % 2)
                 rows = total[k * block : (k + 1) * block].reshape(tensor, own, width)
                 out[pl.ds(at * tensor, tensor), 1 - which] = rows
 
@@ -187,7 +188,7 @@
 
 
 def shards(tokens, w1, b1, w2, b2, pictures, matching, sharpness, offset):
-    axes = ("yl", "core", "t", IMAGE_GROUP[1])
+    axes = ("yl", "core", "t", "xh")
     yl, core, t, xbit = (lax.axis_index(a).astype(jnp.int32) for a in axes)
     place = jnp.stack([yl, core, t, xbit])
     rows, width = pictures.shape
@@ -215,7 +216,7 @@
     parts = lax.all_to_all(partial, "t", 0, 0)
     couple = jnp.concatenate([packed, moved], axis=0)
     copies = call(text_kernel, bf16((groups, own, width)), (parts,))
-    moved = swap(couple, IMAGE_GROUP[1])
+    moved = swap(couple, "xh")
     image_own = jnp.concatenate([couple, moved], axis=0)
     image_other = swap(image_own, "core")
     text_own = lax.all_to_all(copies, TEXT_GROUP, 0, 0)

time: 98.7 us -> 96.3 us (0.976)
  starting transfers between devices: 42.1 us -> 41 us
    ppermute x4, starting transfers between devices: 19.7 us -> 18.6 us  [swap(): return lax.ppermute(block, axis, [(0, 1), (1, 0)])]
  transfers between devices with their start and end apart: 7 -> 7, of which waited for: 4 -> 4; matrix products, arithmetic and copies ran while one was open for 2% -> 2% of each run, Pallas kernels for 6% -> 7%
where the time goes in v7:
time: 96.3 us; the launch traced here: 95.6 us
  starting transfers between devices  41 us (43%)
  blocking collectives  26.7 us (28%)
  waiting for transfers between devices  12.6 us (13%)
  Pallas kernels  8.61 us (9%)
  local copies, waits for them, and re-layouts  3.1 us (3%)
  between operations  2.03 us (2%)
  other arithmetic  1.59 us (2%)
    all_to_all x1, blocking collectives, shards(): shares = lax.all_to_all(shares, ALL, 0, 0, axis_index_groups=grad_groups())  24.7 us
    ppermute x4, starting transfers between devices, swap(): return lax.ppermute(block, axis, [(0, 1), (1, 0)])  18.6 us
    all_to_all x1, starting transfers between devices, shards(): text_own = lax.all_to_all(copies, TEXT_GROUP, 0, 0)  11.3 us
    pallas_call x6, Pallas kernels, call(): pl.pallas_call(kernel, out_shape=outs, in_specs=specs or [SMEM] * scalars...  8.61 us
    all_to_all x1, starting transfers between devices, shards(): gathered = lax.all_to_all(to_all, 't', 0, 0)  7.64 us
    all_to_all x1, waiting for transfers between devices, shards(): text_own = lax.all_to_all(copies, TEXT_GROUP, 0, 0)  6.53 us
    all_to_all x1, starting transfers between devices, shards(): parts = lax.all_to_all(partial, 't', 0, 0)  3.37 us
    all_to_all x1, waiting for transfers between devices, shards(): gathered = lax.all_to_all(to_all, 't', 0, 0)  3.36 us
  transfers between devices with their start and end apart: 7, of which 4 were waited for; matrix products, arithmetic and copies ran while one was open for 2% of the time, Pallas kernels for 7%

profile of v7, /device:TPU:1, one launch (start us, length us, event | category | flops | bytes accessed | tf_op | source)
XLA Modules:
  0.0 95.6 jit_solution(2605172933644315776)
XLA Ops:
  0.6 1.5 %broadcast_in_dim.4 = bf16[4,64,288]{2,1,0:T(8,128)(2,1)} broadcast(bf16[64,288]{1,0:T(8,128)(2,1)} %param.9), dimensions={1,2} | broadcast | bytes 184320 | tf_op jit(solution)/shard_map/broadcast_in_dim | solution.py:200
  2.1 7.6 %all-to-all-start = ((bf16[4,64,288]{2,1,0:T(8,128)(2,1)}), bf16[4,64,288]{2,1,0:T(8,128)(2,1)S(1)}, u32[]{:S(2)}, u32[]{:S(2)}) async-start(bf16[4,64,288]{2,1,0:T(8,128)(2,1)} %broadcast_in_dim.4), calls=%async_computation | async-start | bytes 393216 | tf_op jit(solution)/shard_map/all_to_all | solution.py:201
  9.8 0.7 convert_element_type.5
  10.4 0.7 fusion
  11.1 0.0 copy-start
  11.1 0.9 copy-done
  12.0 0.1 shard_map.106
  12.2 2.3 %collective-permute-start = (bf16[64,1280]{1,0:T(8,128)(2,1)S(1)}, bf16[64,1280]{1,0:T(8,128)(2,1)S(1)}, u32[]{:S(2)}, u32[]{:S(2)}) collective-permute-start(bf16[64,1280]{1,0:T(8,128)(2,1)S(1)} %shard_map.106), channel_id=1, source_target_pairs={{0,256},{256,0},{1,257},{257,1},{2,258},{258,2},{3,259},{259,3},{4... | collective-permute-start | bytes 491528 | tf_op jit(solution)/shard_map/ppermute | solution.py:47
  14.5 3.4 %all-to-all-done.gathered = bf16[4,64,288]{2,1,0:T(8,128)(2,1)S(1)} async-done(((bf16[4,64,288]{2,1,0:T(8,128)(2,1)}), bf16[4,64,288]{2,1,0:T(8,128)(2,1)S(1)}, u32[]{:S(2)}, u32[]{:S(2)}) %all-to-all-start) | async-done | bytes 147488 | tf_op jit(solution)/shard_map/all_to_all | solution.py:201
  17.9 3.2 %shard_map.104 = bf16[4,16,1152]{2,1,0:T(8,128)(2,1)} custom-call(bf16[4,64,288]{2,1,0:T(8,128)(2,1)S(1)} %all-to-all-done.gathered, f32[1,2048]{1,0:T(1,128)S(1)} %bitcast.10, bf16[1152,768]{1,0:T(8,128)(2,1)} %w1.1, bf16[768,1152]{1,0:T(8,128)(2,1)} %w2.1), custom_call_target="tpu_custom_call" | custom-call | bytes 100000 | tf_op jit(solution)/shard_map/pallas_call | solution.py:35
  21.1 3.4 %all-to-all-start.1 = ((bf16[4,16,1152]{2,1,0:T(8,128)(2,1)}), bf16[4,16,1152]{2,1,0:T(8,128)(2,1)S(1)}, u32[]{:S(2)}, u32[]{:S(2)}) async-start(bf16[4,16,1152]{2,1,0:T(8,128)(2,1)} %shard_map.104), calls=%async_computation.1 | async-start | bytes 294912 | tf_op jit(solution)/shard_map/all_to_all | solution.py:216
  24.4 0.0 collective-permute-done
  24.5 4.9 %collective-permute-start.1 = (bf16[128,1280]{1,0:T(8,128)(2,1)S(1)}, bf16[128,1280]{1,0:T(8,128)(2,1)S(1)}, u32[]{:S(2)}, u32[]{:S(2)}) collective-permute-start(bf16[128,1280]{1,0:T(8,128)(2,1)S(1)} %pad_maximum_fusion.1), channel_id=1, source_target_pairs={{0,16},{16,0},{1,17},{17,1},{2,18},{18,2},{3,19},{19,3},{4,20},{20... | collective-permute-start | bytes 983048 | tf_op jit(solution)/shard_map/ppermute | solution.py:47
  29.4 2.5 %all-to-all-done.1.parts = bf16[4,16,1152]{2,1,0:T(8,128)(2,1)S(1)} async-done(((bf16[4,16,1152]{2,1,0:T(8,128)(2,1)}), bf16[4,16,1152]{2,1,0:T(8,128)(2,1)S(1)}, u32[]{:S(2)}, u32[]{:S(2)}) %all-to-all-start.1) | async-done | bytes 147488 | tf_op jit(solution)/shard_map/all_to_all | solution.py:216
  31.9 1.0 %shard_map.105 = bf16[16,16,1152]{2,1,0:T(8,128)(2,1)} custom-call(bf16[4,16,1152]{2,1,0:T(8,128)(2,1)S(1)} %all-to-all-done.1.parts), custom_call_target="tpu_custom_call" | custom-call | bytes 100000 | tf_op jit(solution)/shard_map/pallas_call | solution.py:35
  32.8 11.3 %all-to-all-start.2 = ((bf16[16,16,1152]{2,1,0:T(8,128)(2,1)}), bf16[16,16,1152]{2,1,0:T(8,128)(2,1)S(1)}, u32[]{:S(2)}, u32[]{:S(2)}) async-start(bf16[16,16,1152]{2,1,0:T(8,128)(2,1)} %shard_map.105), calls=%async_computation.2 | async-start | bytes 1179648 | tf_op jit(solution)/shard_map/all_to_all | solution.py:222
  44.2 0.0 collective-permute-done.1
  44.2 5.3 %collective-permute-start.2 = (bf16[256,1280]{1,0:T(8,128)(2,1)S(1)}, bf16[256,1280]{1,0:T(8,128)(2,1)S(1)}, u32[]{:S(2)}, u32[]{:S(2)}) collective-permute-start(bf16[256,1280]{1,0:T(8,128)(2,1)S(1)} %pad_maximum_fusion.image_own), channel_id=1, source_target_pairs={{0,4},{4,0},{1,5},{5,1},{2,6},{6,2},{3,7},{7,3},{8,12},{12,8},{9,1... | collective-permute-start | bytes 1966088 | tf_op jit(solution)/shard_map/ppermute | solution.py:47
  50.8 0.1 pad_maximum_fusion.2.numbers
  50.9 0.1 pad_add_fusion.place
  51.0 0.2 collective-permute-done.2.image_other
  51.2 6.5 %all-to-all-done.2.text = bf16[16,16,1152]{2,1,0:T(8,128)(2,1)S(1)} async-done(((bf16[16,16,1152]{2,1,0:T(8,128)(2,1)}), bf16[16,16,1152]{2,1,0:T(8,128)(2,1)S(1)}, u32[]{:S(2)}, u32[]{:S(2)}) %all-to-all-start.2) | async-done | bytes 589856 | tf_op jit(solution)/shard_map/all_to_all | solution.py:222
  57.8 6.1 %collective-permute-start.3 = (bf16[16,16,1152]{2,1,0:T(8,128)(2,1)S(1)}, bf16[16,16,1152]{2,1,0:T(8,128)(2,1)S(1)}, u32[]{:S(2)}, u32[]{:S(2)}) collective-permute-start(bf16[16,16,1152]{2,1,0:T(8,128)(2,1)S(1)} %all-to-all-done.2.text), channel_id=1, source_target_pairs={{0,4},{4,0},{1,5},{5,1},{2,6},{6,2},{3,7},{7,3},{8,12},{12,8},{9,1... | collective-permute-start | bytes 1769480 | tf_op jit(solution)/shard_map/ppermute | solution.py:47
  63.9 2.1 %shard_map.107.held = f32[2,256,1152]{2,1,0:T(8,128)S(1)} custom-call(s32[4]{0:T(128)S(1)} %pad_add_fusion.place, f32[2]{0:T(128)S(1)} %pad_maximum_fusion.2.numbers, bf16[16,16,1152]{2,1,0:T(8,128)(2,1)S(1)} %all-to-all-done.2.text, bf16[256,1280]{1,0:T(8,128)(2,1)S(1)} %pad_maximum_fusion.image_own, bf16[256,1280]{1,0:T(8,128)(2,1)S(1)} %collective-permute-done.2.image_other), custom_call_target="tpu_custom_call" | custom-call | flops 600000000 | bytes 100000 | tf_op jit(solution)/shard_map/pallas_call | solution.py:35
  65.9 0.0 collective-permute-done.3.text
  66.0 2.1 %shard_map.108 = bf16[16,2,16,1152]{3,2,1,0:T(8,128)(2,1)S(1)} custom-call(s32[4]{0:T(128)S(1)} %pad_add_fusion.place, f32[2]{0:T(128)S(1)} %pad_maximum_fusion.2.numbers, bf16[16,16,1152]{2,1,0:T(8,128)(2,1)S(1)} %collective-permute-done.3.text, bf16[256,1280]{1,0:T(8,128)(2,1)S(1)} %pad_maximum_fusion.image_own, ...), custom_call_target="tpu_custom_call" | custom-call | flops 600000000 | bytes 100000 | tf_op jit(solution)/shard_map/pallas_call | solution.py:35
  68.1 24.7 %all_to_all.20.parts = bf16[16,2,16,1152]{3,2,1,0:T(8,128)(2,1)S(1)} all-to-all(bf16[16,2,16,1152]{3,2,1,0:T(8,128)(2,1)S(1)} %shard_map.108), channel_id=1, replica_groups={{0,32,64,96,128,160,192,224,8,40,72,104,136,168,200,232},{1,33,65,97,12..., dimensions={0} | all-to-all | bytes 2359296 | tf_op jit(solution)/shard_map/all_to_all | solution.py:241
  92.7 0.2 shard_map.109
  92.9 2.0 %all-gather = f32[4,16,1152]{2,1,0:T(8,128)S(1)} all-gather(f32[2,16,1152]{2,1,0:T(8,128)S(1)} %shard_map.109), channel_id=2, replica_groups=mesh['yl'=2,'z'=8,'xh'=2,'xl'=2,'core'=2,'t'=4] {'core'}, dimensions={0}, use_global_device_ids=true | all-gather | bytes 442368 | tf_op jit(solution)/shard_map/all_gather | solution.py:243
  94.9 0.7 dynamic-slice_bitcast_fusion
  (3 shorter events, 0.1 us)
Async XLA Ops:
  2.1 15.7 %all-to-all-start = ((bf16[4,64,288]{2,1,0:T(8,128)(2,1)}), bf16[4,64,288]{2,1,0:T(8,128)(2,1)S(1)}, u32[]{:S(2)}, u32[]{:S(2)}) async-start(bf16[4,64,288]{2,1,0:T(8,128)(2,1)} %broadcast_in_dim.4), calls=%async_computation | async-start | bytes 393216 | tf_op jit(solution)/shard_map/all_to_all | solution.py:201
  11.1 0.9 copy-start
  12.2 12.3 %collective-permute-start = (bf16[64,1280]{1,0:T(8,128)(2,1)S(1)}, bf16[64,1280]{1,0:T(8,128)(2,1)S(1)}, u32[]{:S(2)}, u32[]{:S(2)}) collective-permute-start(bf16[64,1280]{1,0:T(8,128)(2,1)S(1)} %shard_map.106), channel_id=1, source_target_pairs={{0,256},{256,0},{1,257},{257,1},{2,258},{258,2},{3,259},{259,3},{4... | collective-permute-start | bytes 491528 | tf_op jit(solution)/shard_map/ppermute | solution.py:47
  21.1 10.8 %all-to-all-start.1 = ((bf16[4,16,1152]{2,1,0:T(8,128)(2,1)}), bf16[4,16,1152]{2,1,0:T(8,128)(2,1)S(1)}, u32[]{:S(2)}, u32[]{:S(2)}) async-start(bf16[4,16,1152]{2,1,0:T(8,128)(2,1)} %shard_map.104), calls=%async_computation.1 | async-start | bytes 294912 | tf_op jit(solution)/shard_map/all_to_all | solution.py:216
  24.5 19.7 %collective-permute-start.1 = (bf16[128,1280]{1,0:T(8,128)(2,1)S(1)}, bf16[128,1280]{1,0:T(8,128)(2,1)S(1)}, u32[]{:S(2)}, u32[]{:S(2)}) collective-permute-start(bf16[128,1280]{1,0:T(8,128)(2,1)S(1)} %pad_maximum_fusion.1), channel_id=1, source_target_pairs={{0,16},{16,0},{1,17},{17,1},{2,18},{18,2},{3,19},{19,3},{4,20},{20... | collective-permute-start | bytes 983048 | tf_op jit(solution)/shard_map/ppermute | solution.py:47
  32.8 24.9 %all-to-all-start.2 = ((bf16[16,16,1152]{2,1,0:T(8,128)(2,1)}), bf16[16,16,1152]{2,1,0:T(8,128)(2,1)S(1)}, u32[]{:S(2)}, u32[]{:S(2)}) async-start(bf16[16,16,1152]{2,1,0:T(8,128)(2,1)} %shard_map.105), calls=%async_computation.2 | async-start | bytes 1179648 | tf_op jit(solution)/shard_map/all_to_all | solution.py:222
  44.2 7.0 %collective-permute-start.2 = (bf16[256,1280]{1,0:T(8,128)(2,1)S(1)}, bf16[256,1280]{1,0:T(8,128)(2,1)S(1)}, u32[]{:S(2)}, u32[]{:S(2)}) collective-permute-start(bf16[256,1280]{1,0:T(8,128)(2,1)S(1)} %pad_maximum_fusion.image_own), channel_id=1, source_target_pairs={{0,4},{4,0},{1,5},{5,1},{2,6},{6,2},{3,7},{7,3},{8,12},{12,8},{9,1... | collective-permute-start | bytes 1966088 | tf_op jit(solution)/shard_map/ppermute | solution.py:47
  57.8 8.2 %collective-permute-start.3 = (bf16[16,16,1152]{2,1,0:T(8,128)(2,1)S(1)}, bf16[16,16,1152]{2,1,0:T(8,128)(2,1)S(1)}, u32[]{:S(2)}, u32[]{:S(2)}) collective-permute-start(bf16[16,16,1152]{2,1,0:T(8,128)(2,1)S(1)} %all-to-all-done.2.text), channel_id=1, source_target_pairs={{0,4},{4,0},{1,5},{5,1},{2,6},{6,2},{3,7},{7,3},{8,12},{12,8},{9,1... | collective-permute-start | bytes 1769480 | tf_op jit(solution)/shard_map/ppermute | solution.py:47

commit v8 on v7

--- a/solution.py
+++ b/solution.py
@@ -17,6 +17,7 @@
 BF16 = jnp.bfloat16
 F32 = jnp.float32
 LANES = 128
+CHUNKS = 4
 VMEM = pl.BlockSpec(memory_space=pltpu.VMEM)
 HBM = pl.BlockSpec(memory_space=pl.ANY)
 FULL = 55_000_000
@@ -81,10 +82,18 @@
 
 
 def ffn_kernel(gathered, small, w1, w2, partial, w1_near, w2_near, sems):
-    first = pltpu.make_async_copy(w1, w1_near, sems.at[0])
-    second = pltpu.make_async_copy(w2, w2_near, sems.at[1])
-    first.start()
-    second.start()
+    def fetch(far, near, base):
+        step = far.shape[0] // CHUNKS
+        copies = []
+        for k in range(CHUNKS):
+            part = pl.ds(k * step, step)
+            copies.append(pltpu.make_async_copy(far.at[part], near.at[part], sems.at[base + k]))
+        for copy in copies:
+            copy.start()
+        return copies
+
+    first = fetch(w1, w1_near, 0)
+    second = fetch(w2, w2_near, CHUNKS)
     hid = w1.shape[1]
     b1, b2 = small[:, LANES : LANES + hid], small[:, LANES + hid :]
     count = gathered.shape[0]
@@ -92,9 +101,11 @@
     centred = tokens - jnp.mean(tokens, axis=-1, keepdims=True)
     variance = jnp.mean(centred * centred, axis=-1, keepdims=True)
     normed = (centred * lax.rsqrt(variance + EPSILON)).astype(BF16)
-    first.wait()
+    for copy in first:
+        copy.wait()
     hidden = jax.nn.gelu(nn(normed, w1_near[...]) + b1, approximate=True).astype(BF16)
-    second.wait()
+    for copy in second:
+        copy.wait()
     branch = nn(hidden, w2_near[...])
     total = branch + (tokens + b2) * (1.0 / count)
     partial[...] = total.reshape(partial.shape).astype(partial.dtype)
@@ -210,7 +221,7 @@
         (gathered, small, w1, w2),
         specs=[VMEM, VMEM, HBM, HBM],
         scratch=[pltpu.VMEM(a.shape, a.dtype) for a in (w1, w2)]
-        + [pltpu.SemaphoreType.DMA((2,))],
+        + [pltpu.SemaphoreType.DMA((2 * CHUNKS,))],
         room=FULL,
     )
     parts = lax.all_to_all(partial, "t", 0, 0)

time: 96.3 us -> 96.3 us (level)
  no operation moved by 1% of the time
where the time goes in v8:
time: 96.3 us; the launch traced here: 95.6 us
  starting transfers between devices  40.9 us (42%)
  blocking collectives  26.7 us (28%)
  waiting for transfers between devices  12.6 us (13%)
  Pallas kernels  8.64 us (9%)
  local copies, waits for them, and re-layouts  3.1 us (3%)
  between operations  2.03 us (2%)
  other arithmetic  1.59 us (2%)
    all_to_all x1, blocking collectives, shards(): shares = lax.all_to_all(shares, ALL, 0, 0, axis_index_groups=grad_groups())  24.7 us
    ppermute x4, starting transfers between devices, swap(): return lax.ppermute(block, axis, [(0, 1), (1, 0)])  18.6 us
    all_to_all x1, starting transfers between devices, shards(): text_own = lax.all_to_all(copies, TEXT_GROUP, 0, 0)  11.3 us
    pallas_call x6, Pallas kernels, call(): pl.pallas_call(kernel, out_shape=outs, in_specs=specs or [SMEM] * scalars...  8.64 us
    all_to_all x1, starting transfers between devices, shards(): gathered = lax.all_to_all(to_all, 't', 0, 0)  7.64 us
    all_to_all x1, waiting for transfers between devices, shards(): text_own = lax.all_to_all(copies, TEXT_GROUP, 0, 0)  6.55 us
    all_to_all x1, starting transfers between devices, shards(): parts = lax.all_to_all(partial, 't', 0, 0)  3.38 us
    all_to_all x1, waiting for transfers between devices, shards(): gathered = lax.all_to_all(to_all, 't', 0, 0)  3.36 us
  transfers between devices with their start and end apart: 7, of which 4 were waited for; matrix products, arithmetic and copies ran while one was open for 2% of the time, Pallas kernels for 7%

profile of v8, /device:TPU:1, one launch (start us, length us, event | category | flops | bytes accessed | tf_op | source)
XLA Modules:
  0.0 95.6 jit_solution(7715034516544111082)
XLA Ops:
  0.6 1.5 %broadcast_in_dim.4 = bf16[4,64,288]{2,1,0:T(8,128)(2,1)} broadcast(bf16[64,288]{1,0:T(8,128)(2,1)} %param.9), dimensions={1,2} | broadcast | bytes 184320 | tf_op jit(solution)/shard_map/broadcast_in_dim | solution.py:211
  2.1 7.6 %all-to-all-start = ((bf16[4,64,288]{2,1,0:T(8,128)(2,1)}), bf16[4,64,288]{2,1,0:T(8,128)(2,1)S(1)}, u32[]{:S(2)}, u32[]{:S(2)}) async-start(bf16[4,64,288]{2,1,0:T(8,128)(2,1)} %broadcast_in_dim.4), calls=%async_computation | async-start | bytes 393216 | tf_op jit(solution)/shard_map/all_to_all | solution.py:212
  9.8 0.7 convert_element_type.5
  10.4 0.7 fusion
  11.1 0.0 copy-start
  11.1 0.9 copy-done
  12.0 0.1 shard_map.106
  12.2 2.3 %collective-permute-start = (bf16[64,1280]{1,0:T(8,128)(2,1)S(1)}, bf16[64,1280]{1,0:T(8,128)(2,1)S(1)}, u32[]{:S(2)}, u32[]{:S(2)}) collective-permute-start(bf16[64,1280]{1,0:T(8,128)(2,1)S(1)} %shard_map.106), channel_id=1, source_target_pairs={{0,256},{256,0},{1,257},{257,1},{2,258},{258,2},{3,259},{259,3},{4... | collective-permute-start | bytes 491528 | tf_op jit(solution)/shard_map/ppermute | solution.py:48
  14.5 3.4 %all-to-all-done.gathered = bf16[4,64,288]{2,1,0:T(8,128)(2,1)S(1)} async-done(((bf16[4,64,288]{2,1,0:T(8,128)(2,1)}), bf16[4,64,288]{2,1,0:T(8,128)(2,1)S(1)}, u32[]{:S(2)}, u32[]{:S(2)}) %all-to-all-start) | async-done | bytes 147488 | tf_op jit(solution)/shard_map/all_to_all | solution.py:212
  17.9 3.2 %shard_map.104 = bf16[4,16,1152]{2,1,0:T(8,128)(2,1)} custom-call(bf16[4,64,288]{2,1,0:T(8,128)(2,1)S(1)} %all-to-all-done.gathered, f32[1,2048]{1,0:T(1,128)S(1)} %bitcast.10, bf16[1152,768]{1,0:T(8,128)(2,1)} %w1.1, bf16[768,1152]{1,0:T(8,128)(2,1)} %w2.1), custom_call_target="tpu_custom_call" | custom-call | bytes 100000 | tf_op jit(solution)/shard_map/pallas_call | solution.py:36
  21.1 3.4 %all-to-all-start.1 = ((bf16[4,16,1152]{2,1,0:T(8,128)(2,1)}), bf16[4,16,1152]{2,1,0:T(8,128)(2,1)S(1)}, u32[]{:S(2)}, u32[]{:S(2)}) async-start(bf16[4,16,1152]{2,1,0:T(8,128)(2,1)} %shard_map.104), calls=%async_computation.1 | async-start | bytes 294912 | tf_op jit(solution)/shard_map/all_to_all | solution.py:227
  24.5 0.0 collective-permute-done
  24.5 4.9 %collective-permute-start.1 = (bf16[128,1280]{1,0:T(8,128)(2,1)S(1)}, bf16[128,1280]{1,0:T(8,128)(2,1)S(1)}, u32[]{:S(2)}, u32[]{:S(2)}) collective-permute-start(bf16[128,1280]{1,0:T(8,128)(2,1)S(1)} %pad_maximum_fusion.1), channel_id=1, source_target_pairs={{0,16},{16,0},{1,17},{17,1},{2,18},{18,2},{3,19},{19,3},{4,20},{20... | collective-permute-start | bytes 983048 | tf_op jit(solution)/shard_map/ppermute | solution.py:48
  29.4 2.5 %all-to-all-done.1.parts = bf16[4,16,1152]{2,1,0:T(8,128)(2,1)S(1)} async-done(((bf16[4,16,1152]{2,1,0:T(8,128)(2,1)}), bf16[4,16,1152]{2,1,0:T(8,128)(2,1)S(1)}, u32[]{:S(2)}, u32[]{:S(2)}) %all-to-all-start.1) | async-done | bytes 147488 | tf_op jit(solution)/shard_map/all_to_all | solution.py:227
  31.9 1.0 %shard_map.105 = bf16[16,16,1152]{2,1,0:T(8,128)(2,1)} custom-call(bf16[4,16,1152]{2,1,0:T(8,128)(2,1)S(1)} %all-to-all-done.1.parts), custom_call_target="tpu_custom_call" | custom-call | bytes 100000 | tf_op jit(solution)/shard_map/pallas_call | solution.py:36
  32.9 11.3 %all-to-all-start.2 = ((bf16[16,16,1152]{2,1,0:T(8,128)(2,1)}), bf16[16,16,1152]{2,1,0:T(8,128)(2,1)S(1)}, u32[]{:S(2)}, u32[]{:S(2)}) async-start(bf16[16,16,1152]{2,1,0:T(8,128)(2,1)} %shard_map.105), calls=%async_computation.2 | async-start | bytes 1179648 | tf_op jit(solution)/shard_map/all_to_all | solution.py:233
  44.2 0.0 collective-permute-done.1
  44.3 5.3 %collective-permute-start.2 = (bf16[256,1280]{1,0:T(8,128)(2,1)S(1)}, bf16[256,1280]{1,0:T(8,128)(2,1)S(1)}, u32[]{:S(2)}, u32[]{:S(2)}) collective-permute-start(bf16[256,1280]{1,0:T(8,128)(2,1)S(1)} %pad_maximum_fusion.image_own), channel_id=1, source_target_pairs={{0,4},{4,0},{1,5},{5,1},{2,6},{6,2},{3,7},{7,3},{8,12},{12,8},{9,1... | collective-permute-start | bytes 1966088 | tf_op jit(solution)/shard_map/ppermute | solution.py:48
  50.9 0.1 pad_maximum_fusion.2.numbers
  51.0 0.1 pad_add_fusion.place
  51.0 0.2 collective-permute-done.2.image_other
  51.3 6.6 %all-to-all-done.2.text = bf16[16,16,1152]{2,1,0:T(8,128)(2,1)S(1)} async-done(((bf16[16,16,1152]{2,1,0:T(8,128)(2,1)}), bf16[16,16,1152]{2,1,0:T(8,128)(2,1)S(1)}, u32[]{:S(2)}, u32[]{:S(2)}) %all-to-all-start.2) | async-done | bytes 589856 | tf_op jit(solution)/shard_map/all_to_all | solution.py:233
  57.8 6.1 %collective-permute-start.3 = (bf16[16,16,1152]{2,1,0:T(8,128)(2,1)S(1)}, bf16[16,16,1152]{2,1,0:T(8,128)(2,1)S(1)}, u32[]{:S(2)}, u32[]{:S(2)}) collective-permute-start(bf16[16,16,1152]{2,1,0:T(8,128)(2,1)S(1)} %all-to-all-done.2.text), channel_id=1, source_target_pairs={{0,4},{4,0},{1,5},{5,1},{2,6},{6,2},{3,7},{7,3},{8,12},{12,8},{9,1... | collective-permute-start | bytes 1769480 | tf_op jit(solution)/shard_map/ppermute | solution.py:48
  63.9 2.1 %shard_map.107.held = f32[2,256,1152]{2,1,0:T(8,128)S(1)} custom-call(s32[4]{0:T(128)S(1)} %pad_add_fusion.place, f32[2]{0:T(128)S(1)} %pad_maximum_fusion.2.numbers, bf16[16,16,1152]{2,1,0:T(8,128)(2,1)S(1)} %all-to-all-done.2.text, bf16[256,1280]{1,0:T(8,128)(2,1)S(1)} %pad_maximum_fusion.image_own, bf16[256,1280]{1,0:T(8,128)(2,1)S(1)} %collective-permute-done.2.image_other), custom_call_target="tpu_custom_call" | custom-call | flops 600000000 | bytes 100000 | tf_op jit(solution)/shard_map/pallas_call | solution.py:36
  66.0 0.0 collective-permute-done.3.text
  66.0 2.1 %shard_map.108 = bf16[16,2,16,1152]{3,2,1,0:T(8,128)(2,1)S(1)} custom-call(s32[4]{0:T(128)S(1)} %pad_add_fusion.place, f32[2]{0:T(128)S(1)} %pad_maximum_fusion.2.numbers, bf16[16,16,1152]{2,1,0:T(8,128)(2,1)S(1)} %collective-permute-done.3.text, bf16[256,1280]{1,0:T(8,128)(2,1)S(1)} %pad_maximum_fusion.image_own, ...), custom_call_target="tpu_custom_call" | custom-call | flops 600000000 | bytes 100000 | tf_op jit(solution)/shard_map/pallas_call | solution.py:36
  68.1 24.7 %all_to_all.20.parts = bf16[16,2,16,1152]{3,2,1,0:T(8,128)(2,1)S(1)} all-to-all(bf16[16,2,16,1152]{3,2,1,0:T(8,128)(2,1)S(1)} %shard_map.108), channel_id=1, replica_groups={{0,32,64,96,128,160,192,224,8,40,72,104,136,168,200,232},{1,33,65,97,12..., dimensions={0} | all-to-all | bytes 2359296 | tf_op jit(solution)/shard_map/all_to_all | solution.py:252
  92.8 0.2 shard_map.109
  92.9 2.0 %all-gather = f32[4,16,1152]{2,1,0:T(8,128)S(1)} all-gather(f32[2,16,1152]{2,1,0:T(8,128)S(1)} %shard_map.109), channel_id=2, replica_groups=mesh['yl'=2,'z'=8,'xh'=2,'xl'=2,'core'=2,'t'=4] {'core'}, dimensions={0}, use_global_device_ids=true | all-gather | bytes 442368 | tf_op jit(solution)/shard_map/all_gather | solution.py:254
  95.0 0.7 dynamic-slice_bitcast_fusion
  (3 shorter events, 0.1 us)
Async XLA Ops:
  2.1 15.7 %all-to-all-start = ((bf16[4,64,288]{2,1,0:T(8,128)(2,1)}), bf16[4,64,288]{2,1,0:T(8,128)(2,1)S(1)}, u32[]{:S(2)}, u32[]{:S(2)}) async-start(bf16[4,64,288]{2,1,0:T(8,128)(2,1)} %broadcast_in_dim.4), calls=%async_computation | async-start | bytes 393216 | tf_op jit(solution)/shard_map/all_to_all | solution.py:212
  11.1 0.9 copy-start
  12.2 12.3 %collective-permute-start = (bf16[64,1280]{1,0:T(8,128)(2,1)S(1)}, bf16[64,1280]{1,0:T(8,128)(2,1)S(1)}, u32[]{:S(2)}, u32[]{:S(2)}) collective-permute-start(bf16[64,1280]{1,0:T(8,128)(2,1)S(1)} %shard_map.106), channel_id=1, source_target_pairs={{0,256},{256,0},{1,257},{257,1},{2,258},{258,2},{3,259},{259,3},{4... | collective-permute-start | bytes 491528 | tf_op jit(solution)/shard_map/ppermute | solution.py:48
  21.1 10.8 %all-to-all-start.1 = ((bf16[4,16,1152]{2,1,0:T(8,128)(2,1)}), bf16[4,16,1152]{2,1,0:T(8,128)(2,1)S(1)}, u32[]{:S(2)}, u32[]{:S(2)}) async-start(bf16[4,16,1152]{2,1,0:T(8,128)(2,1)} %shard_map.104), calls=%async_computation.1 | async-start | bytes 294912 | tf_op jit(solution)/shard_map/all_to_all | solution.py:227
  24.5 19.7 %collective-permute-start.1 = (bf16[128,1280]{1,0:T(8,128)(2,1)S(1)}, bf16[128,1280]{1,0:T(8,128)(2,1)S(1)}, u32[]{:S(2)}, u32[]{:S(2)}) collective-permute-start(bf16[128,1280]{1,0:T(8,128)(2,1)S(1)} %pad_maximum_fusion.1), channel_id=1, source_target_pairs={{0,16},{16,0},{1,17},{17,1},{2,18},{18,2},{3,19},{19,3},{4,20},{20... | collective-permute-start | bytes 983048 | tf_op jit(solution)/shard_map/ppermute | solution.py:48
  32.9 25.0 %all-to-all-start.2 = ((bf16[16,16,1152]{2,1,0:T(8,128)(2,1)}), bf16[16,16,1152]{2,1,0:T(8,128)(2,1)S(1)}, u32[]{:S(2)}, u32[]{:S(2)}) async-start(bf16[16,16,1152]{2,1,0:T(8,128)(2,1)} %shard_map.105), calls=%async_computation.2 | async-start | bytes 1179648 | tf_op jit(solution)/shard_map/all_to_all | solution.py:233
  44.3 7.0 %collective-permute-start.2 = (bf16[256,1280]{1,0:T(8,128)(2,1)S(1)}, bf16[256,1280]{1,0:T(8,128)(2,1)S(1)}, u32[]{:S(2)}, u32[]{:S(2)}) collective-permute-start(bf16[256,1280]{1,0:T(8,128)(2,1)S(1)} %pad_maximum_fusion.image_own), channel_id=1, source_target_pairs={{0,4},{4,0},{1,5},{5,1},{2,6},{6,2},{3,7},{7,3},{8,12},{12,8},{9,1... | collective-permute-start | bytes 1966088 | tf_op jit(solution)/shard_map/ppermute | solution.py:48
  57.8 8.1 %collective-permute-start.3 = (bf16[16,16,1152]{2,1,0:T(8,128)(2,1)S(1)}, bf16[16,16,1152]{2,1,0:T(8,128)(2,1)S(1)}, u32[]{:S(2)}, u32[]{:S(2)}) collective-permute-start(bf16[16,16,1152]{2,1,0:T(8,128)(2,1)S(1)} %all-to-all-done.2.text), channel_id=1, source_target_pairs={{0,4},{4,0},{1,5},{5,1},{2,6},{6,2},{3,7},{7,3},{8,12},{12,8},{9,1... | collective-permute-start | bytes 1769480 | tf_op jit(solution)/shard_map/ppermute | solution.py:48
